TPU v7x, 256 devices: a whole 4x4x8 slice. The times are simulated.
256 devices in a mesh: dom: 64 (over x, z, core), hid: 4 (over y).
Axes of the slice: x: 4, y: 4, z: 8, core: 2. Of those that a mesh axis runs over, the one named last changes fastest.
Arguments:
- feat: bfloat16 [16384, 1024], P('dom', 'hid'), may hold values from -6 to 6
- cotangent: bfloat16 [16384, 1024], P('dom', 'hid'), may hold values from -6 to 6
- tiles: bfloat16 [64, 32, 128, 128], P('dom')
- tile_index: int32 [64, 32], P('dom'), may hold values from 0 to 35, as said below
- tile_count: int32 [64], P('dom'), may hold values from 6 to 32, as said below
- replica_slot: int32 [64, 512], P('dom'), may hold values from 0 to 255, as said below
- recv_count: int32 [64, 64], P('dom'), may hold values from 0 to 8, as said below
- w_self1: bfloat16 [1024, 1024], P(None, 'hid'), may hold values from -0.1875 to 0.1875
- w_neigh1: bfloat16 [1024, 1024], P(None, 'hid'), may hold values from -0.1875 to 0.1875
- w_self2: bfloat16 [1024, 1024], P(None, 'hid'), may hold values from -0.1875 to 0.1875
- w_neigh2: bfloat16 [1024, 1024], P(None, 'hid'), may hold values from -0.1875 to 0.1875
Outputs:
- output: bfloat16 [16384, 1024], P('dom', 'hid')
- grad_self1: float32 [1024, 1024], P(None, 'hid')
- grad_neigh1: float32 [1024, 1024], P(None, 'hid')
- grad_self2: float32 [1024, 1024], P(None, 'hid')
- grad_neigh2: float32 [1024, 1024], P(None, 'hid')
Inputs may be any that keep to these rules, and one draw needn't show every extreme that they name: `tile_index`: entries of one partition are distinct; entry e names the tile at block row e // 6 and block column e % 6; the first 6 entries of every partition are its diagonal tiles in some order. Partition d uses its first tile_count[d] tile slots; some partition uses all 32. `replica_slot`: entry p * 8 + c of owner d is the master row held in mirror slot c of partition p; the 8 entries for one partition are distinct. `recv_count`: entry [d, p] says how many of the first mirror slots for owner d on partition p are live; it is zero for p = d, and every owner has a partition with all 8 live.
All inputs are finite; a program needn't handle non-finite values.
Results may differ from a plain program's by a relative error of at most 0.0058.
Values may be sent and summed in bfloat16 or wider, within the bound.
A program may use at most 64 MiB of HBM per device.

v0:
```python
import math

import jax
import jax.numpy as jnp
from jax import lax
from jax.sharding import PartitionSpec as P


def local(
    feat,
    cotangent,
    tiles,
    tile_index,
    tile_count,
    replica_slot,
    recv_count,
    w_self1,
    w_neigh1,
    w_self2,
    w_neigh2,
):
    groups = lax.axis_size("dom")
    masters = feat.shape[0]
    narrow = feat.shape[1]
    mirrors = replica_slot.shape[1]
    slots = mirrors // groups
    tile_size = tiles.shape[2]
    block_count = (masters + mirrors) // tile_size
    slot_list = replica_slot[0]
    live_mask = (jnp.arange(slots, dtype=jnp.int32)[None, :] < recv_count[0][:, None]).reshape(
        mirrors, 1
    )
    tile_values = tiles[0]
    tile_slots = tile_index[0]
    block_rows = tile_slots // block_count
    block_cols = tile_slots % block_count
    active = (jnp.arange(tile_slots.shape[0], dtype=jnp.int32) < tile_count[0]).astype(jnp.float32)
    block_ids = jnp.arange(block_count, dtype=jnp.int32)
    row_select = (block_rows[None, :] == block_ids[:, None]).astype(jnp.float32) * active[None, :]
    col_select = (block_cols[None, :] == block_ids[:, None]).astype(jnp.float32) * active[None, :]

    def to_mirrors(values):
        outgoing = jnp.where(live_mask, values[slot_list], jnp.zeros((), values.dtype))
        incoming = lax.all_to_all(
            outgoing.reshape(groups, slots, narrow), "dom", split_axis=0, concat_axis=0, tiled=True
        )
        return incoming.reshape(mirrors, narrow)

    def to_masters(master_part, mirror_part):
        incoming = lax.all_to_all(
            mirror_part.reshape(groups, slots, narrow),
            "dom",
            split_axis=0,
            concat_axis=0,
            tiled=True,
        )
        arrived = jnp.where(
            live_mask,
            incoming.reshape(mirrors, narrow).astype(jnp.float32),
            jnp.zeros((), jnp.float32),
        )
        return master_part.at[slot_list].add(arrived)

    def propagate(local_field, transpose):
        blocked = local_field.reshape(block_count, tile_size, narrow)
        if transpose:
            product = jnp.einsum(
                "tji,tjq->tiq", tile_values, blocked[block_rows], preferred_element_type=jnp.float32
            )
            select = col_select
        else:
            product = jnp.einsum(
                "tij,tjq->tiq", tile_values, blocked[block_cols], preferred_element_type=jnp.float32
            )
            select = row_select
        result = jnp.einsum("bt,tiq->biq", select, product, precision=lax.Precision.HIGHEST)
        return result.reshape(block_count * tile_size, narrow)

    def aggregate(values, transpose):
        local_field = jnp.concatenate([values, to_mirrors(values)], axis=0)
        partial_sum = propagate(local_field, transpose)
        return to_masters(partial_sum[:masters], partial_sum[masters:].astype(jnp.bfloat16))

    def project(values, summed, w_self, w_neigh):
        full_values, full_summed = (
            lax.all_gather(values, "hid", axis=1, tiled=True),
            lax.all_gather(summed, "hid", axis=1, tiled=True),
        )
        pre_act = jnp.dot(full_values, w_self, preferred_element_type=jnp.float32) + jnp.dot(
            full_summed, w_neigh, preferred_element_type=jnp.float32
        )
        return (pre_act, full_values, full_summed)

    agg_one = aggregate(feat, False).astype(jnp.bfloat16)
    pre_one, full_feat, full_agg_one = project(feat, agg_one, w_self1, w_neigh1)
    hidden_one = jax.nn.silu(pre_one).astype(jnp.bfloat16)
    agg_two = aggregate(hidden_one, False).astype(jnp.bfloat16)
    pre_two, full_hidden, full_agg_two = project(hidden_one, agg_two, w_self2, w_neigh2)
    output = pre_two.astype(jnp.bfloat16)
    grad_self2 = jnp.einsum("mi,mj->ij", full_hidden, cotangent, preferred_element_type=jnp.float32)
    grad_neigh2 = jnp.einsum(
        "mi,mj->ij", full_agg_two, cotangent, preferred_element_type=jnp.float32
    )
    back_hidden, back_agg = (
        lax.psum_scatter(
            jnp.dot(cotangent, w_self2.T, preferred_element_type=jnp.float32),
            "hid",
            scatter_dimension=1,
            tiled=True,
        ),
        lax.psum_scatter(
            jnp.dot(cotangent, w_neigh2.T, preferred_element_type=jnp.float32),
            "hid",
            scatter_dimension=1,
            tiled=True,
        ),
    )
    back_hidden = lax.optimization_barrier(back_hidden.astype(jnp.bfloat16))
    back_agg = back_agg.astype(jnp.bfloat16)
    adjoint = aggregate(back_agg, True)
    back_one = back_hidden.astype(jnp.float32) + adjoint
    sigma = jax.nn.sigmoid(pre_one)
    back_pre = (back_one * sigma * (1.0 + pre_one * (1.0 - sigma))).astype(jnp.bfloat16)
    grad_self1 = jnp.einsum("mi,mj->ij", full_feat, back_pre, preferred_element_type=jnp.float32)
    grad_neigh1 = jnp.einsum(
        "mi,mj->ij", full_agg_one, back_pre, preferred_element_type=jnp.float32
    )
    grad_self1, grad_neigh1, grad_self2, grad_neigh2 = lax.psum(
        (grad_self1, grad_neigh1, grad_self2, grad_neigh2), "dom"
    )
    factor = 1.0 / math.sqrt(groups * masters)
    return (
        output,
        grad_self1 * factor,
        grad_neigh1 * factor,
        grad_self2 * factor,
        grad_neigh2 * factor,
    )


def solution(mesh):
    in_specs = (
        P("dom", "hid"),
        P("dom", "hid"),
        P("dom", None, None, None),
        P("dom", None),
        P("dom"),
        P("dom", None),
        P("dom", None),
        P(None, "hid"),
        P(None, "hid"),
        P(None, "hid"),
        P(None, "hid"),
    )
    out_specs = (P("dom", "hid"), P(None, "hid"), P(None, "hid"), P(None, "hid"), P(None, "hid"))
    return jax.shard_map(local, mesh=mesh, in_specs=in_specs, out_specs=out_specs, check_vma=False)
```

profile of v0, /device:TPU:1, one launch (start us, length us, event | category | flops | bytes accessed | tf_op | source)
XLA Modules:
  0.0 454.0 jit_solution(12300040357161135217)
XLA Ops:
  7.2 2.5 fusion.51
  9.9 1.3 fusion.50
  12.0 2.0 gather_fusion
  14.0 25.7 %reduce-scatter.5.cloned.1.call-done = f32[256,256]{1,0:T(8,128)} async-done(((f32[256,1024]{1,0:T(8,128)}), f32[256,256]{1,0:T(8,128)}) %reduce-scatter.5.cloned.1.call-update) | async-done | bytes 262160 | tf_op jit(solution)/shard_map/reduce_scatter | solution.py:111
  39.7 1.0 convert_element_type.79
  40.6 2.0 gather_fusion.4
  42.6 0.9 bitcast_select_fusion
  43.5 12.1 %all-to-all-start = ((bf16[64,8,256]{2,1,0:T(8,128)(2,1)}), bf16[64,8,256]{2,1,0:T(8,128)(2,1)S(1)}, u32[]{:S(2)}, u32[]{:S(2)}) async-start(bf16[64,8,256]{2,1,0:T(8,128)(2,1)} %get-tuple-element.24), calls=%async_computation | async-start | bytes 524288 | tf_op jit(solution)/shard_map/all_to_all | solution.py:44
  55.6 13.6 %all_gather.12 = bf16[256,1024]{1,0:T(8,128)(2,1)S(1)} all-gather(bf16[256,256]{1,0:T(8,128)(2,1)S(1)} %copy-done.1), channel_id=1, replica_groups=mesh['dom'=64,'hid'=4] {'hid'}, dimensions={1}, use_global_device_ids=true | all-gather | bytes 655360 | tf_op jit(solution)/shard_map/all_gather | solution.py:86
  69.2 12.4 %all-to-all-start.4 = ((bf16[64,8,256]{2,1,0:T(8,128)(2,1)}), bf16[64,8,256]{2,1,0:T(8,128)(2,1)}, u32[]{:S(2)}, u32[]{:S(2)}) async-start(bf16[64,8,256]{2,1,0:T(8,128)(2,1)} %get-tuple-element.23), calls=%async_computation.6 | async-start | bytes 524288 | tf_op jit(solution)/shard_map/all_to_all | solution.py:44
  81.6 2.0 gather_fusion.1
  83.7 4.3 fusion.11
  88.0 5.5 %copy.37 = f32[32,256,128]{1,0,2:T(8,128)} copy(f32[32,256,128]{2,1,0:T(8,128)} %fusion.11) | data formatting | bytes 8388608 | tf_op jit(solution)/shard_map/tij,tjq->tiq/dot_general | solution.py:72
  93.5 3.8 fusion.4
  97.3 0.1 slice.65
  97.5 0.7 copy.25
  98.2 10.5 %all-to-all-start.1 = ((bf16[64,8,256]{2,1,0:T(8,128)(2,1)}), bf16[64,8,256]{2,1,0:T(8,128)(2,1)}, u32[]{:S(2)}, u32[]{:S(2)}) async-start(bf16[64,8,256]{2,1,0:T(8,128)(2,1)} %bitcast.14), calls=%async_computation.1 | async-start | bytes 524288 | tf_op jit(solution)/shard_map/all_to_all | solution.py:50
  108.7 1.0 pad_maximum_fusion.2
  109.7 2.0 gather_fusion.5
  111.7 4.3 fusion.7
  116.0 5.5 %copy.39 = f32[32,256,128]{1,0,2:T(8,128)} copy(f32[32,256,128]{2,1,0:T(8,128)} %fusion.7) | data formatting | bytes 8388608 | tf_op jit(solution)/shard_map/tji,tjq->tiq/dot_general | solution.py:67
  121.6 3.8 fusion
  125.4 1.0 copy-done.2
  126.4 0.1 slice.63
  126.5 0.7 copy.29
  127.3 10.5 %all-to-all-start.5 = ((bf16[64,8,256]{2,1,0:T(8,128)(2,1)}), bf16[64,8,256]{2,1,0:T(8,128)(2,1)}, u32[]{:S(2)}, u32[]{:S(2)}) async-start(bf16[64,8,256]{2,1,0:T(8,128)(2,1)} %bitcast.33), calls=%async_computation.7 | async-start | bytes 524288 | tf_op jit(solution)/shard_map/all_to_all | solution.py:50
  137.8 2.0 fusion.48
  139.9 1.0 convert_element_type.77
  141.1 4.0 scatter_custom_fusion
  145.1 10.1 %all_gather.13 = bf16[256,1024]{1,0:T(8,128)(2,1)S(1)} all-gather(bf16[256,256]{1,0:T(8,128)(2,1)S(1)} %convert_element_type.70), channel_id=1, replica_groups=mesh['dom'=64,'hid'=4] {'hid'}, dimensions={1}, use_global_device_ids=true | all-gather | bytes 655360 | tf_op jit(solution)/shard_map/all_gather | solution.py:87
  155.2 4.0 scatter_custom_fusion.2
  159.2 1.4 multiply_convert_fusion
  160.6 2.0 gather_fusion.2
  162.6 0.8 bitcast_select_fusion.1
  163.4 13.7 %all-to-all-start.2 = ((bf16[64,8,256]{2,1,0:T(8,128)(2,1)}), bf16[64,8,256]{2,1,0:T(8,128)(2,1)S(1)}, u32[]{:S(2)}, u32[]{:S(2)}) async-start(bf16[64,8,256]{2,1,0:T(8,128)(2,1)} %bitcast_select_fusion.1), calls=%async_computation.2 | async-start | bytes 524288 | tf_op jit(solution)/shard_map/all_to_all | solution.py:44
  177.1 10.8 %all_gather.14 = bf16[256,1024]{1,0:T(8,128)(2,1)S(1)} all-gather(bf16[256,256]{1,0:T(8,128)(2,1)S(1)} %get-tuple-element.22), channel_id=1, replica_groups=mesh['dom'=64,'hid'=4] {'hid'}, dimensions={1}, use_global_device_ids=true | all-gather | bytes 655360 | tf_op jit(solution)/shard_map/all_gather | solution.py:86
  187.9 1.3 fusion.52
  189.2 2.0 gather_fusion.3
  191.2 4.3 fusion.9
  195.5 5.5 %copy.38 = f32[32,256,128]{1,0,2:T(8,128)} copy(f32[32,256,128]{2,1,0:T(8,128)} %fusion.9) | data formatting | bytes 8388608 | tf_op jit(solution)/shard_map/tij,tjq->tiq/dot_general | solution.py:72
  201.1 3.8 fusion.2
  204.9 1.0 copy-done.3
  205.9 0.1 slice.64
  206.0 0.7 copy.27
  206.8 13.0 %all-to-all-start.3 = ((bf16[64,8,256]{2,1,0:T(8,128)(2,1)}), bf16[64,8,256]{2,1,0:T(8,128)(2,1)S(1)}, u32[]{:S(2)}, u32[]{:S(2)}) async-start(bf16[64,8,256]{2,1,0:T(8,128)(2,1)} %bitcast.21), calls=%async_computation.3 | async-start | bytes 524288 | tf_op jit(solution)/shard_map/all_to_all | solution.py:50
  219.8 0.3 all-reduce.3.cloned.1.call-start
  220.1 1.3 convolution_bitcast_fusion
  221.4 1.3 fusion.53
  222.7 9.1 %all-to-all-done.3 = bf16[64,8,256]{2,1,0:T(8,128)(2,1)S(1)} async-done(((bf16[64,8,256]{2,1,0:T(8,128)(2,1)}), bf16[64,8,256]{2,1,0:T(8,128)(2,1)S(1)}, u32[]{:S(2)}, u32[]{:S(2)}) %all-to-all-start.3) | async-done | bytes 262176 | tf_op jit(solution)/shard_map/all_to_all | solution.py:50
  231.8 3.6 scatter_custom_fusion.1
  235.4 9.9 %all_gather.15 = bf16[256,1024]{1,0:T(8,128)(2,1)S(1)} all-gather(bf16[256,256]{1,0:T(8,128)(2,1)S(1)} %convert_element_type.75), channel_id=1, replica_groups=mesh['dom'=64,'hid'=4] {'hid'}, dimensions={1}, use_global_device_ids=true | all-gather | bytes 655360 | tf_op jit(solution)/shard_map/all_gather | solution.py:87
  245.3 1.3 fusion.54
  246.6 1.0 copy-done.5
  247.6 0.3 fusion.49
  248.0 1.0 fusion.6
  248.9 190.3 %all-reduce.3.cloned.1.call-done = (f32[1024,256]{0,1:T(8,128)}, f32[1024,256]{0,1:T(8,128)}, f32[1024,256]{0,1:T(8,128)}, f32[1024,256]{0,1:T(8,128)}) async-done(((f32[1024,256]{0,1:T(8,128)}, f32[1024,256]{0,1:T(8,128)}, f32[1024,256]{0,1:T(8,128)}, f32[1024,256]{0,1:T(8,128)}), (f32[1024,256]{0,1:T(8,128)}, f32[1024,256]{0,1:T(8,128)}, f32[1024,256]{0,1:T(8,128)}, ...) | async-done | bytes 4194320 | tf_op jit(solution)/shard_map/psum | solution.py:128
  439.2 1.4 broadcast_multiply_fusion.3
  440.6 1.3 copy.33
  441.9 0.1 broadcast_multiply_fusion.2
  442.0 1.3 copy.34
  443.3 1.4 broadcast_multiply_fusion.1
  444.7 1.3 copy.35
  446.0 0.1 broadcast_multiply_fusion
  446.2 1.3 copy.36
  (57 shorter events, 0.7 us)
Async XLA Ops:
  7.2 76.5 %copy-start = (bf16[1,32,128,128]{3,2,1,0:T(8,128)(2,1)S(1)}, bf16[1,32,128,128]{3,2,1,0:T(8,128)(2,1)}, u32[]{:S(2)}) copy-start(bf16[1,32,128,128]{3,2,1,0:T(8,128)(2,1)} %param.13) | copy-start | bytes 3145732
  7.2 2.7 copy-start.7
  7.2 2.7 copy-start.4
  7.2 32.5 %reduce-scatter.5.cloned.1.call-start = ((), (), s32[]{:S(2)}) async-start(), calls=%async_computation.9 | async-start | bytes 1310720 | tf_op jit(solution)/shard_map/reduce_scatter | solution.py:111
  9.8 1.4 copy-start.11
  9.8 1.5 copy-start.13
  9.8 1.6 copy-start.12
  9.8 2.2 copy-start.1
  9.8 130.1 %reduce-scatter.3.cloned.1.call-start = ((), (), s32[]{:S(2)}) async-start(), calls=%async_computation.8 | async-start | bytes 1310720 | tf_op jit(solution)/shard_map/reduce_scatter | solution.py:105
  43.5 25.7 %all-to-all-start = ((bf16[64,8,256]{2,1,0:T(8,128)(2,1)}), bf16[64,8,256]{2,1,0:T(8,128)(2,1)S(1)}, u32[]{:S(2)}, u32[]{:S(2)}) async-start(bf16[64,8,256]{2,1,0:T(8,128)(2,1)} %get-tuple-element.24), calls=%async_computation | async-start | bytes 524288 | tf_op jit(solution)/shard_map/all_to_all | solution.py:44
  69.2 29.0 %all-to-all-start.4 = ((bf16[64,8,256]{2,1,0:T(8,128)(2,1)}), bf16[64,8,256]{2,1,0:T(8,128)(2,1)}, u32[]{:S(2)}, u32[]{:S(2)}) async-start(bf16[64,8,256]{2,1,0:T(8,128)(2,1)} %get-tuple-element.23), calls=%async_computation.6 | async-start | bytes 524288 | tf_op jit(solution)/shard_map/all_to_all | solution.py:44
  98.2 29.0 %all-to-all-start.1 = ((bf16[64,8,256]{2,1,0:T(8,128)(2,1)}), bf16[64,8,256]{2,1,0:T(8,128)(2,1)}, u32[]{:S(2)}, u32[]{:S(2)}) async-start(bf16[64,8,256]{2,1,0:T(8,128)(2,1)} %bitcast.14), calls=%async_computation.1 | async-start | bytes 524288 | tf_op jit(solution)/shard_map/all_to_all | solution.py:50
  125.4 1.0 copy-start.2
  126.5 14.5 %slice-start = ((f32[6,128,256]{2,0,1:T(8,128)}), f32[2,128,256]{2,0,1:T(2,128)S(1)}, s32[]{:S(2)}) async-start(f32[6,128,256]{2,0,1:T(8,128)} %copy-done.2), calls=%async_computation.11 | async-start | bytes 524288 | tf_op jit(solution)/shard_map/slice | solution.py:82
  127.3 27.9 %all-to-all-start.5 = ((bf16[64,8,256]{2,1,0:T(8,128)(2,1)}), bf16[64,8,256]{2,1,0:T(8,128)(2,1)}, u32[]{:S(2)}, u32[]{:S(2)}) async-start(bf16[64,8,256]{2,1,0:T(8,128)(2,1)} %bitcast.33), calls=%async_computation.7 | async-start | bytes 524288 | tf_op jit(solution)/shard_map/all_to_all | solution.py:50
  141.0 18.2 %copy-start.10 = (f32[256,256]{1,0:T(8,128)S(1)}, f32[256,256]{1,0:T(8,128)}, u32[]{:S(2)}) copy-start(f32[256,256]{1,0:T(8,128)} %fusion.48) | copy-start | bytes 786436
  163.4 25.8 %all-to-all-start.2 = ((bf16[64,8,256]{2,1,0:T(8,128)(2,1)}), bf16[64,8,256]{2,1,0:T(8,128)(2,1)S(1)}, u32[]{:S(2)}, u32[]{:S(2)}) async-start(bf16[64,8,256]{2,1,0:T(8,128)(2,1)} %bitcast_select_fusion.1), calls=%async_computation.2 | async-start | bytes 524288 | tf_op jit(solution)/shard_map/all_to_all | solution.py:44
  204.9 1.0 copy-start.3
  206.8 15.9 %slice-start.1 = ((f32[6,128,256]{2,0,1:T(8,128)}), f32[2,128,256]{2,0,1:T(2,128)S(1)}, s32[]{:S(2)}) async-start(f32[6,128,256]{2,0,1:T(8,128)} %copy-done.3), calls=%async_computation.12 | async-start | bytes 524288 | tf_op jit(solution)/shard_map/slice | solution.py:82
  206.8 25.0 %all-to-all-start.3 = ((bf16[64,8,256]{2,1,0:T(8,128)(2,1)}), bf16[64,8,256]{2,1,0:T(8,128)(2,1)S(1)}, u32[]{:S(2)}, u32[]{:S(2)}) async-start(bf16[64,8,256]{2,1,0:T(8,128)(2,1)} %bitcast.21), calls=%async_computation.3 | async-start | bytes 524288 | tf_op jit(solution)/shard_map/all_to_all | solution.py:50
  219.8 219.4 %all-reduce.3.cloned.1.call-start = ((), (), s32[]{:S(2)}) async-start(), calls=%async_computation.10 | async-start | bytes 8388608 | tf_op jit(solution)/shard_map/psum | solution.py:128
  246.6 1.0 copy-start.5
  246.6 1.3 copy-start.6
  439.2 2.7 copy-start.9
  443.3 2.7 copy-start.8
Sparse Core Ops, SparseCore 0:
  11.2 28.4 reduce-scatter.4
  43.0 28.8 reduce-scatter.2
  246.7 192.4 all-reduce.2
where the time goes:
time: 456 us; the launch traced here: 454 us
  waiting for transfers between devices  225 us (49%)
  starting transfers between devices  72.5 us (16%)
  blocking collectives  44.3 us (10%)
  local copies, waits for them, and re-layouts  39.6 us (9%)
  matrix products  38.1 us (8%)
  other arithmetic  19.4 us (4%)
  between operations  14.9 us (3%)
    psum x1, waiting for transfers between devices, local(): lax.psum((grad_self1, grad_neigh1, grad_self2, grad_neigh2), 'dom')  190 us
    all_to_all x3, starting transfers between devices, to_mirrors(): lax.all_to_all(outgoing.reshape(groups, slots, narrow), 'dom', split_axis...  38.1 us
    all_to_all x3, starting transfers between devices, to_masters(): lax.all_to_all(mirror_part.reshape(groups, slots, narrow), 'dom', split_a...  34.1 us
    reduce_scatter x1, waiting for transfers between devices, local(): lax.psum_scatter(jnp.dot(cotangent, w_neigh2.T, preferred_element_type=jn...  25.7 us
    all_gather x2, blocking collectives, project(): lax.all_gather(values, 'hid', axis=1, tiled=True)  24.4 us
    all_gather x2, blocking collectives, project(): lax.all_gather(summed, 'hid', axis=1, tiled=True)  20 us
    scatter-add x3, other arithmetic, to_masters(): return master_part.at[slot_list].add(arrived)  11.5 us
    dot_general x3, matrix products, propagate(): jnp.einsum('bt,tiq->biq', select, product, precision=lax.Precision.HIGHEST)  11.5 us
  transfers between devices with their start and end apart: 9, of which 3 were waited for; matrix products, arithmetic and copies ran while one was open for 12% of the time, Pallas kernels for 0%

commit v1 on v0

v1 whole, which is shorter than its diff:
```python
import math

import jax
import jax.numpy as jnp
from jax import lax
from jax.experimental import pallas as pl
from jax.experimental.pallas import tpu as pltpu
from jax.sharding import PartitionSpec as P

BF = jnp.bfloat16
F32 = jnp.float32
I32 = jnp.int32
LANES = 128
CHIPS_Z = 8


def dot(a, b):
    return jnp.dot(a, b, preferred_element_type=F32)


def dot_t(a, b):
    return lax.dot_general(a, b, (((0,), (0,)), ((), ())), preferred_element_type=F32)


def dot_r(a, b):
    return lax.dot_general(a, b, (((1,), (1,)), ((), ())), preferred_element_type=F32)


def pack(rows, slots):
    count, width = rows.shape
    parts = [
        rows[:, i : i + LANES].reshape(count // slots, slots, LANES) for i in range(0, width, LANES)
    ]
    return jnp.concatenate(parts, axis=1).astype(BF)


def unpack(packed, slots):
    wide = packed.astype(F32)
    groups, rows, _ = wide.shape
    parts = [
        wide[:, i : i + slots, :].reshape(groups * slots, LANES) for i in range(0, rows, slots)
    ]
    return jnp.concatenate(parts, axis=1).astype(BF)


def kernel(
    dims,
    slot_of,
    used,
    feat,
    cot,
    slot_row,
    counts,
    tiles,
    ws1,
    wn1,
    ws2,
    wn2,
    out,
    gout,
    tiles_v,
    w_v,
    onehot,
    onehot_t,
    adj,
    adj_t,
    send1,
    recv1,
    send2,
    recv2,
    send3,
    recv3,
    send4,
    recv4,
    left,
    hid_all,
    right,
    back_f32,
    rs_send,
    rs_recv,
    pre_v,
    own_v,
    acc,
    s0s,
    s0r,
    s1s,
    s1r,
    own1,
    s2s,
    s2r,
    fin,
    lsem,
    esem,
    ersem,
    ysem,
    yrsem,
    gsem,
    grsem,
):
    doms, hids, slots, masters, narrow = dims
    chips_z = CHIPS_Z
    chips_x = doms // (2 * chips_z)
    size = tiles.shape[1]
    mirrors = doms * slots
    blocks = (masters + mirrors) // size
    width = hids * narrow
    me = lax.axis_index("dom")
    hid = lax.axis_index("hid")
    core = lax.rem(me, 2)
    chip = me // 2
    cx, cz = chip // chips_z, lax.rem(chip, chips_z)

    def remote(src, dst, ssem, rsem, **where):
        return pltpu.make_async_remote_copy(
            src_ref=src,
            dst_ref=dst,
            send_sem=ssem,
            recv_sem=rsem,
            device_id=where,
            device_id_type=pl.DeviceIdType.MESH,
        )

    barrier = pltpu.get_barrier_semaphore()

    def greet(i, carry):
        pl.semaphore_signal(
            barrier,
            inc=1,
            device_id={"dom": lax.rem(me + i, doms)},
            device_id_type=pl.DeviceIdType.MESH,
        )
        return carry

    lax.fori_loop(1, doms, greet, 0)
    for i in range(1, hids):
        pl.semaphore_signal(
            barrier,
            inc=1,
            device_id={"hid": lax.rem(hid + i, hids)},
            device_id_type=pl.DeviceIdType.MESH,
        )

    loads = [pltpu.make_async_copy(tiles, tiles_v, lsem.at[0])]
    for i, w in enumerate((ws1, ws2, wn1, wn2)):
        loads.append(pltpu.make_async_copy(w, w_v.at[i], lsem.at[i + 1]))
    for load in loads:
        load.start()

    grp = lax.broadcasted_iota(I32, (doms, mirrors), 0)
    col = lax.broadcasted_iota(I32, (doms, mirrors), 1)
    repeat = (col // slots == grp).astype(F32)
    live_count = dot(jnp.broadcast_to(counts[...].astype(F32), (8, doms)), repeat)[0:1]
    lane = lax.broadcasted_iota(I32, (1, mirrors), 1)
    live = lax.rem(lane, slots).astype(F32) + 0.5 < live_count
    slot = jnp.where(live, slot_row[...], -1)
    row = lax.broadcasted_iota(I32, (masters, mirrors), 0)
    hot = (row == slot).astype(F32)
    onehot_t[...] = hot.astype(BF)
    onehot[...] = hot.T.astype(BF)

    send1[...] = pack(dot(onehot[...], jnp.concatenate([feat[...], cot[...]], axis=1)), slots)
    for buf in (recv1, recv2, recv3, recv4):
        buf[me] = jnp.zeros(buf.shape[1:], BF)
    left[0, hid] = feat[...]
    right[0] = cot[...]

    pl.semaphore_wait(barrier, doms - 1 + hids - 1)

    def exchange_start(n, src, dst):
        def one(i, carry):
            peer = lax.rem(me + i, doms)
            remote(src.at[peer], dst.at[me], esem.at[n], ersem.at[n], dom=peer).start()
            return carry

        lax.fori_loop(1, doms, one, 0)

    def exchange_wait(n, src, dst):
        some = pl.ds(0, doms - 1)
        done = remote(
            src.at[some], dst.at[some], esem.at[n], ersem.at[n], dom=lax.rem(me + 1, doms)
        )
        done.wait_recv()
        done.wait_send()

    def gather_start(n, src, dst):
        for i in range(1, hids):
            remote(src, dst, ysem.at[n], yrsem.at[n], hid=lax.rem(hid + i, hids)).start()

    def gather_wait(n, src, dst):
        some = pl.ds(0, hids - 1)
        done = remote(src.at[some], dst.at[some], ysem.at[n], yrsem.at[n], hid=lax.rem(hid + 1, hids))
        done.wait_recv()
        done.wait_send()

    exchange_start(0, send1, recv1)
    gather_start(0, feat, left.at[0, hid])

    loads[0].wait()
    for r in range(blocks):
        for c in range(blocks):
            e = r * blocks + c
            tile = jnp.where(used[e] > 0, tiles_v[slot_of[e]], jnp.zeros((), BF))
            rs, cs = pl.ds(r * size, size), pl.ds(c * size, size)
            adj[rs, cs] = tile
            adj_t[cs, rs] = tile.astype(F32).T.astype(BF)

    for load in loads[1:]:
        load.wait()

    def block(h):
        return pl.ds(h * narrow, narrow)

    for h in range(hids):
        back_f32[h] = dot_r(cot[...], w_v[1, block(h)])

    top, low = pl.ds(0, masters), pl.ds(masters, mirrors)
    exchange_wait(0, send1, recv1)
    held = unpack(recv1[...], slots)
    fwd, bwd = held[:, :narrow], held[:, narrow:]
    mirror = jnp.concatenate(
        [
            dot(adj[low, top], feat[...]) + dot(adj[low, low], fwd),
            dot(adj_t[low, top], cot[...]) + dot(adj_t[low, low], bwd),
        ],
        axis=1,
    )
    send2[...] = pack(mirror, slots)
    exchange_start(1, send2, recv2)
    own_v[0] = dot(adj[top, top], feat[...]) + dot(adj[top, low], fwd)
    own_v[1] = dot(adj_t[top, top], cot[...]) + dot(adj_t[top, low], bwd)

    gather_wait(0, left.at[0], left.at[0])
    pre = dot(left[0, 0], w_v[0, block(0)])
    for h in range(1, hids):
        pre += dot(left[0, h], w_v[0, block(h)])
    pre_v[...] = pre

    exchange_wait(1, send2, recv2)
    back = unpack(recv2[...], slots)
    left[1, hid] = (own_v[0] + dot(onehot_t[...], back[:, :narrow])).astype(BF)
    gather_start(1, left.at[1, hid], left.at[1, hid])
    right[1] = (own_v[1] + dot(onehot_t[...], back[:, narrow:])).astype(BF)
    for h in range(hids):
        rs_send[h] = (back_f32[h] + dot_r(right[1], w_v[3, block(h)])).astype(BF)
    for i in range(1, hids):
        peer = lax.rem(hid + i, hids)
        remote(rs_send.at[peer], rs_recv.at[hid], ysem.at[2], yrsem.at[2], hid=peer).start()

    gather_wait(1, left.at[1], left.at[1])
    pre = pre_v[...]
    for h in range(hids):
        pre += dot(left[1, h], w_v[2, block(h)])
    sigma = jax.nn.sigmoid(pre)
    hid_all[hid] = (pre * sigma).astype(BF)
    gather_start(3, hid_all.at[hid], hid_all.at[hid])

    gather_wait(2, rs_send, rs_recv)
    back_one = rs_send[hid].astype(F32)
    for i in range(1, hids):
        back_one += rs_recv[lax.rem(hid + i, hids)].astype(F32)
    back_pre = (back_one * sigma * (1.0 + pre * (1.0 - sigma))).astype(BF)

    sibling = me + 1 - 2 * core
    piece = width // chips_x
    chunk = piece // chips_z
    factor = 1.0 / math.sqrt(doms * masters)

    def to_sibling(g):
        return remote(s0s.at[g], s0r.at[g], gsem.at[g, 0], grsem.at[g, 0], dom=sibling)

    for h in range(hids):
        s0s[0, block(h)] = dot_t(left[1 - core, h], back_pre).astype(BF)
    to_sibling(0).start()
    for h in range(hids):
        acc[0, block(h)] = dot_t(left[core, h], back_pre)

    gather_wait(3, hid_all, hid_all)
    mixed = dot(hid_all[0], w_v[3, block(0)])
    for h in range(1, hids):
        mixed += dot(hid_all[h], w_v[3, block(h)])
    mixed = mixed.astype(BF)
    send3[...] = pack(dot(onehot[...], mixed), slots)
    exchange_start(2, send3, recv3)

    for h in range(hids):
        s0s[1, block(h)] = dot_t(hid_all[h], right[1 - core]).astype(BF)
    to_sibling(1).start()
    for h in range(hids):
        acc[1, block(h)] = dot_t(hid_all[h], right[core])

    def dom_of(x, z):
        return (x * chips_z + z) * 2 + core

    def x_start(g):
        done = to_sibling(g)
        done.wait_recv()
        done.wait_send()
        s1s[g] = (acc[g] + s0r[g].astype(F32)).astype(BF)
        mine = pl.ds(cx * piece, piece)
        own1[g] = acc[g, mine] + s0r[g, mine].astype(F32)
        for i in range(1, chips_x):
            px = lax.rem(cx + i, chips_x)
            remote(
                s1s.at[g, pl.ds(px * piece, piece)],
                s1r.at[g, cx],
                gsem.at[g, 1],
                grsem.at[g, 1],
                dom=dom_of(px, cz),
            ).start()

    def z_start(g):
        some = pl.ds(0, (chips_x - 1) * piece)
        done = remote(
            s1s.at[g, some], s1s.at[g, some], gsem.at[g, 1], grsem.at[g, 1], dom=sibling
        )
        done.wait_recv()
        done.wait_send()
        total = own1[g]
        for i in range(1, chips_x):
            total += s1r[g, lax.rem(cx + i, chips_x)].astype(F32)
        own1[g] = total
        s2s[g] = total.astype(BF)
        for i in range(1, chips_z):
            pz = lax.rem(cz + i, chips_z)
            remote(
                s2s.at[g, pl.ds(pz * chunk, chunk)],
                s2r.at[g, cz],
                gsem.at[g, 2],
                grsem.at[g, 2],
                dom=dom_of(cx, pz),
            ).start()

    def z_back(g):
        some = pl.ds(0, (chips_z - 1) * chunk)
        done = remote(
            s2s.at[g, some], s2s.at[g, some], gsem.at[g, 2], grsem.at[g, 2], dom=sibling
        )
        done.wait_recv()
        done.wait_send()
        total = own1[g, pl.ds(cz * chunk, chunk)]
        for i in range(1, chips_z):
            total += s2r[g, lax.rem(cz + i, chips_z)].astype(F32)
        fin[g] = (total * factor).astype(BF)
        place = gout.at[g, core, pl.ds(cx * piece + cz * chunk, chunk)]
        pltpu.make_async_copy(fin.at[g], place, lsem.at[5 + g]).start()
        for i in range(1, chips_z):
            pz = lax.rem(cz + i, chips_z)
            remote(fin.at[g], place, gsem.at[g, 3], grsem.at[g, 3], dom=dom_of(cx, pz)).start()

    def x_back(g):
        place = gout.at[g, core, pl.ds(cx * piece + cz * chunk, chunk)]
        pltpu.make_async_copy(fin.at[g], place, lsem.at[5 + g]).wait()
        some = gout.at[g, core, pl.ds(0, (chips_z - 1) * chunk)]
        done = remote(some, some, gsem.at[g, 3], grsem.at[g, 3], dom=sibling)
        done.wait_recv()
        done.wait_send()
        mine = gout.at[g, core, pl.ds(cx * piece, piece)]
        for i in range(1, chips_x):
            px = lax.rem(cx + i, chips_x)
            remote(mine, mine, gsem.at[g, 4], grsem.at[g, 4], dom=dom_of(px, cz)).start()

    def core_back(g):
        some = gout.at[g, core, pl.ds(0, (chips_x - 1) * piece)]
        done = remote(some, some, gsem.at[g, 4], grsem.at[g, 4], dom=sibling)
        done.wait_recv()
        done.wait_send()
        mine = gout.at[g, core]
        remote(mine, mine, gsem.at[g, 5], grsem.at[g, 5], dom=sibling).start()

    x_start(0)

    exchange_wait(2, send3, recv3)
    held = unpack(recv3[...], slots)
    send4[...] = pack(dot(adj[low, top], mixed) + dot(adj[low, low], held), slots)
    exchange_start(3, send4, recv4)
    x_start(1)
    total = dot(adj[top, top], mixed) + dot(adj[top, low], held)
    for h in range(hids):
        total += dot(hid_all[h], w_v[1, block(h)])
    own_v[0] = total

    z_start(0)
    z_back(0)
    exchange_wait(3, send4, recv4)
    out[...] = (own_v[0] + dot(onehot_t[...], unpack(recv4[...], slots))).astype(BF)
    z_start(1)
    x_back(0)
    z_back(1)
    core_back(0)
    x_back(1)
    core_back(1)
    for g in range(2):
        mine = gout.at[g, core]
        done = remote(mine, mine, gsem.at[g, 5], grsem.at[g, 5], dom=sibling)
        done.wait_recv()
        done.wait_send()


def local(
    feat,
    cotangent,
    tiles,
    tile_index,
    tile_count,
    replica_slot,
    recv_count,
    w_self1,
    w_neigh1,
    w_self2,
    w_neigh2,
):
    doms, hids = lax.axis_size("dom"), lax.axis_size("hid")
    masters, narrow = feat.shape
    width = narrow * hids
    mirrors = replica_slot.shape[1]
    slots = mirrors // doms
    size = tiles.shape[2]
    blocks = (masters + mirrors) // size
    side = blocks * size
    chips_x = doms // (2 * CHIPS_Z)
    piece = width // chips_x
    chunk = piece // CHIPS_Z

    order = jnp.arange(tiles.shape[1], dtype=I32)
    match = (
        (tile_index[0][None, :] == jnp.arange(blocks * blocks, dtype=I32)[:, None])
        & (order < tile_count[0])[None, :]
    ).astype(I32)
    slot_of = (match * order[None, :]).sum(axis=1)
    used = match.sum(axis=1)

    packed = slots * narrow // LANES
    smem = pl.BlockSpec(memory_space=pltpu.SMEM)
    vmem = pl.BlockSpec(memory_space=pltpu.VMEM)
    anym = pl.BlockSpec(memory_space=pl.ANY)
    dma = pltpu.SemaphoreType.DMA

    def body(*refs):
        kernel((doms, hids, slots, masters, narrow), *refs)

    out, grads = pl.pallas_call(
        body,
        out_shape=(
            jax.ShapeDtypeStruct((masters, narrow), BF),
            jax.ShapeDtypeStruct((2, 2, width, narrow), BF),
        ),
        in_specs=[smem] * 2 + [vmem] * 4 + [anym] * 5,
        out_specs=(vmem, anym),
        scratch_shapes=[
            pltpu.VMEM(tiles.shape[1:], BF),
            pltpu.VMEM((4, width, narrow), BF),
            pltpu.VMEM((mirrors, masters), BF),
            pltpu.VMEM((masters, mirrors), BF),
            pltpu.VMEM((side, side), BF),
            pltpu.VMEM((side, side), BF),
        ]
        + [pltpu.VMEM((doms, 2 * packed, LANES), BF)] * 4
        + [pltpu.VMEM((doms, packed, LANES), BF)] * 4
        + [
            pltpu.VMEM((2, hids, masters, narrow), BF),
            pltpu.VMEM((hids, masters, narrow), BF),
            pltpu.VMEM((2, masters, narrow), BF),
            pltpu.VMEM((hids, masters, narrow), F32),
            pltpu.VMEM((hids, masters, narrow), BF),
            pltpu.VMEM((hids, masters, narrow), BF),
            pltpu.VMEM((masters, narrow), F32),
            pltpu.VMEM((2, masters, narrow), F32),
            pltpu.VMEM((2, width, narrow), F32),
            pltpu.VMEM((2, width, narrow), BF),
            pltpu.VMEM((2, width, narrow), BF),
            pltpu.VMEM((2, width, narrow), BF),
            pltpu.VMEM((2, chips_x, piece, narrow), BF),
            pltpu.VMEM((2, piece, narrow), F32),
            pltpu.VMEM((2, piece, narrow), BF),
            pltpu.VMEM((2, CHIPS_Z, chunk, narrow), BF),
            pltpu.VMEM((2, chunk, narrow), BF),
            dma((7,)),
            dma((4,)),
            dma((4,)),
            dma((4,)),
            dma((4,)),
            dma((2, 6)),
            dma((2, 6)),
        ],
        compiler_params=pltpu.CompilerParams(
            collective_id=0, has_side_effects=True, vmem_limit_bytes=48 * 1024 * 1024
        ),
    )(
        slot_of,
        used,
        feat,
        cotangent,
        replica_slot,
        recv_count,
        tiles[0],
        w_self1,
        w_neigh1,
        w_self2,
        w_neigh2,
    )
    grads = grads.astype(F32)
    return (out, grads[0, 0], grads[0, 1], grads[1, 0], grads[1, 1])


def solution(mesh):
    rows = P("dom", "hid")
    cols = P(None, "hid")
    return jax.shard_map(
        local,
        mesh=mesh,
        in_specs=(
            rows,
            rows,
            P("dom", None, None, None),
            P("dom", None),
            P("dom"),
            P("dom", None),
            P("dom", None),
            cols,
            cols,
            cols,
            cols,
        ),
        out_specs=(rows, cols, cols, cols, cols),
        check_vma=False,
    )
```

time: 456 us -> 123 us (0.27)
  waiting for transfers between devices: 225 us -> 0 us
  Pallas kernels: 0 us -> 109 us
  starting transfers between devices: 72.5 us -> 0 us
  blocking collectives: 44.3 us -> 0 us
  matrix products: 38.1 us -> 0 us
  local copies, waits for them, and re-layouts: 39.6 us -> 11.3 us
  other arithmetic: 19.4 us -> 1.12 us
  between operations: 14.9 us -> 1.32 us
    psum x1 -> x0, waiting for transfers between devices: 190 us -> none  [local(): lax.psum((grad_self1, grad_neigh1, grad_self2, grad_neigh2), 'dom')]
    pallas_call x0 -> x1, Pallas kernels: none -> 109 us  [local(): pl.pallas_call(body, out_shape=(jax.ShapeDtypeStruct((masters, narrow), B...]
    all_to_all x6 -> x0, starting transfers between devices: 72.2 us -> none  [the longest x3 38.1 us: to_mirrors(): lax.all_to_all(outgoing.reshape(groups, slots, narrow), 'dom', split_axis...]
    all_gather x4 -> x0, blocking collectives: 44.3 us -> none  [the longest x2 24.4 us: project(): lax.all_gather(values, 'hid', axis=1, tiled=True)]
    dot_general x16 -> x0, matrix products: 38.1 us -> none  [the longest x3 11.5 us: propagate(): jnp.einsum('bt,tiq->biq', select, product, precision=lax.Precision.HIGHEST)]
    reduce_scatter x2 -> x0, waiting for transfers between devices: 25.7 us -> none  [the longest x1 25.7 us: local(): lax.psum_scatter(jnp.dot(cotangent, w_neigh2.T, preferred_element_type=jn...]
    dot_general x3 -> x0, local copies, waits for them, and re-layouts: 16.6 us -> none  [the longest x2 11.1 us: propagate(): jnp.einsum('tij,tjq->tiq', tile_values, blocked[block_cols], preferred_el...]
    gather x6 -> x0, local copies, waits for them, and re-layouts: 12 us -> none  [the longest x3 5.86 us: to_mirrors(): values[slot_list]]
  transfers between devices with their start and end apart: 9 -> 0, of which waited for: 3 -> 0; matrix products, arithmetic and copies ran while one was open for 12% -> 0% of each run, Pallas kernels for 0% -> 0%
where the time goes in v1:
time: 123 us
  Pallas kernels  109 us (89%)
  local copies, waits for them, and re-layouts  11.3 us (9%)
  between operations  1.32 us (1%)
    pallas_call x1, Pallas kernels, local(): pl.pallas_call(body, out_shape=(jax.ShapeDtypeStruct((masters, narrow), B...  109 us
    unnamed x19, local copies, waits for them, and re-layouts  9.18 us

profile of v1, /device:TPU:1, one launch (start us, length us, event | category | flops | bytes accessed | tf_op | source)
XLA Modules:
  0.0 122.9 jit_solution(6533644149772090085)
XLA Ops:
  1.3 0.7 convert_reduce_fusion
  2.0 0.0 copy-start
  2.0 1.2 copy-done
  3.3 0.0 copy-start.1
  3.3 1.0 copy-done.1
  4.3 0.0 copy-start.2
  4.3 1.0 copy-done.2
  5.3 0.0 copy-start.3
  5.4 1.0 copy-done.3
  6.4 0.0 copy-start.4
  6.4 1.0 copy-done.4
  7.4 0.0 copy-start.5
  7.4 0.9 copy-done.5
  8.3 0.0 copy-start.6
  8.3 0.9 copy-done.6
  9.2 0.0 copy-start.7
  9.2 0.7 copy-done.7
  9.9 0.0 copy-start.8
  9.9 0.7 copy-done.8
  10.6 109.2 %shard_map.146 = (bf16[256,256]{1,0:T(8,128)(2,1)S(1)}, bf16[2,2,1024,256]{3,2,1,0:T(8,128)(2,1)S(1)}) custom-call(s32[36]{0:T(128)S(1)} %get-tuple-element.10.refs_0_, s32[36]{0:T(128)S(1)} %get-tuple-element.9.refs_1_, bf16[256,256]{1,0:T(8,128)(2,1)S(1)} %copy-done.5, bf16[256,256]{1,0:T(8,128)(2,1)S(1)} %copy-done.6, s32[1,512]{1,0:T(1,128)S(1)} %copy-done.7, ...), custom_call_target="tpu_custom_call" | custom-call | tf_op jit(solution)/shard_map/pallas_call | solution.py:441
  119.8 0.4 convert_element_type.7
  120.1 2.1 %slice_bitcast_fusion = (f32[1024,256]{1,0:T(8,128)}, f32[1024,256]{1,0:T(8,128)}, f32[1024,256]{1,0:T(8,128)}, f32[1024,256]{1,0:T(8,128)}) fusion(f32[2,2,1024,256]{3,2,1,0:T(8,128)S(1)} %convert_element_type.7), kind=kLoop, calls=%fused_computation | loop fusion | bytes 8388608 | tf_op jit(solution)/shard_map/squeeze | solution.py:502
  122.2 0.7 copy.18
  (1 shorter events, 0.0 us)
Async XLA Ops:
  2.0 1.2 copy-start
  3.3 1.0 copy-start.1
  4.3 1.0 copy-start.2
  5.3 1.0 copy-start.3
  6.4 1.0 copy-start.4
  7.4 0.9 copy-start.5
  8.3 0.9 copy-start.6
  9.2 0.7 copy-start.7
  9.9 0.7 copy-start.8

commit v2 on v1

--- a/solution.py
+++ b/solution.py
@@ -64,14 +64,8 @@
     onehot_t,
     adj,
     adj_t,
-    send1,
-    recv1,
-    send2,
-    recv2,
-    send3,
-    recv3,
-    send4,
-    recv4,
+    send,
+    recv,
     left,
     hid_all,
     right,
@@ -85,7 +79,6 @@
     s0r,
     s1s,
     s1r,
-    own1,
     s2s,
     s2r,
     fin,
@@ -95,7 +88,12 @@
     ysem,
     yrsem,
     gsem,
-    grsem,
+    cr_sem,
+    xr_sem,
+    zr_sem,
+    za_sem,
+    xa_sem,
+    ca_sem,
 ):
     doms, hids, slots, masters, narrow = dims
     chips_z = CHIPS_Z
@@ -158,29 +156,31 @@
     onehot_t[...] = hot.astype(BF)
     onehot[...] = hot.T.astype(BF)
 
-    send1[...] = pack(dot(onehot[...], jnp.concatenate([feat[...], cot[...]], axis=1)), slots)
-    for buf in (recv1, recv2, recv3, recv4):
-        buf[me] = jnp.zeros(buf.shape[1:], BF)
+    send[0] = pack(dot(onehot[...], feat[...]), slots)
+    send[1] = pack(dot(onehot[...], cot[...]), slots)
+    for n in range(recv.shape[0]):
+        recv[n, me] = jnp.zeros(recv.shape[2:], BF)
     left[0, hid] = feat[...]
     right[0] = cot[...]
 
     pl.semaphore_wait(barrier, doms - 1 + hids - 1)
 
-    def exchange_start(n, src, dst):
+    def exchange_start(n):
         def one(i, carry):
             peer = lax.rem(me + i, doms)
-            remote(src.at[peer], dst.at[me], esem.at[n], ersem.at[n], dom=peer).start()
+            remote(send.at[n, peer], recv.at[n, me], esem.at[n], ersem.at[n], dom=peer).start()
             return carry
 
         lax.fori_loop(1, doms, one, 0)
 
-    def exchange_wait(n, src, dst):
+    def exchange_wait(n):
         some = pl.ds(0, doms - 1)
         done = remote(
-            src.at[some], dst.at[some], esem.at[n], ersem.at[n], dom=lax.rem(me + 1, doms)
+            send.at[n, some], recv.at[n, some], esem.at[n], ersem.at[n], dom=lax.rem(me + 1, doms)
         )
         done.wait_recv()
         done.wait_send()
+        return unpack(recv[n], slots)
 
     def gather_start(n, src, dst):
         for i in range(1, hids):
@@ -192,8 +192,9 @@
         done.wait_recv()
         done.wait_send()
 
-    exchange_start(0, send1, recv1)
+    exchange_start(0)
     gather_start(0, feat, left.at[0, hid])
+    exchange_start(1)
 
     loads[0].wait()
     for r in range(blocks):
@@ -214,20 +215,15 @@
         back_f32[h] = dot_r(cot[...], w_v[1, block(h)])
 
     top, low = pl.ds(0, masters), pl.ds(masters, mirrors)
-    exchange_wait(0, send1, recv1)
-    held = unpack(recv1[...], slots)
-    fwd, bwd = held[:, :narrow], held[:, narrow:]
-    mirror = jnp.concatenate(
-        [
-            dot(adj[low, top], feat[...]) + dot(adj[low, low], fwd),
-            dot(adj_t[low, top], cot[...]) + dot(adj_t[low, low], bwd),
-        ],
-        axis=1,
-    )
-    send2[...] = pack(mirror, slots)
-    exchange_start(1, send2, recv2)
-    own_v[0] = dot(adj[top, top], feat[...]) + dot(adj[top, low], fwd)
-    own_v[1] = dot(adj_t[top, top], cot[...]) + dot(adj_t[top, low], bwd)
+    held = exchange_wait(0)
+    send[2] = pack(dot(adj[low, top], feat[...]) + dot(adj[low, low], held), slots)
+    exchange_start(2)
+    own_v[0] = dot(adj[top, top], feat[...]) + dot(adj[top, low], held)
+
+    held = exchange_wait(1)
+    send[3] = pack(dot(adj_t[low, top], cot[...]) + dot(adj_t[low, low], held), slots)
+    exchange_start(3)
+    own_v[1] = dot(adj_t[top, top], cot[...]) + dot(adj_t[top, low], held)
 
     gather_wait(0, left.at[0], left.at[0])
     pre = dot(left[0, 0], w_v[0, block(0)])
@@ -235,11 +231,9 @@
         pre += dot(left[0, h], w_v[0, block(h)])
     pre_v[...] = pre
 
-    exchange_wait(1, send2, recv2)
-    back = unpack(recv2[...], slots)
-    left[1, hid] = (own_v[0] + dot(onehot_t[...], back[:, :narrow])).astype(BF)
+    left[1, hid] = (own_v[0] + dot(onehot_t[...], exchange_wait(2))).astype(BF)
     gather_start(1, left.at[1, hid], left.at[1, hid])
-    right[1] = (own_v[1] + dot(onehot_t[...], back[:, narrow:])).astype(BF)
+    right[1] = (own_v[1] + dot(onehot_t[...], exchange_wait(3))).astype(BF)
     for h in range(hids):
         rs_send[h] = (back_f32[h] + dot_r(right[1], w_v[3, block(h)])).astype(BF)
     for i in range(1, hids):
@@ -264,136 +258,139 @@
     piece = width // chips_x
     chunk = piece // chips_z
     factor = 1.0 / math.sqrt(doms * masters)
+    z_order = sorted(range(chips_z), key=lambda j: -min(j, chips_z - j))
+
+    def dom_of(x, z):
+        return (x * chips_z + z) * 2 + core
 
     def to_sibling(g):
-        return remote(s0s.at[g], s0r.at[g], gsem.at[g, 0], grsem.at[g, 0], dom=sibling)
+        return remote(s0s.at[g], s0r.at[g], gsem.at[g, 0], cr_sem.at[g], dom=sibling)
+
+    def x_start(g):
+        done = to_sibling(g)
+        done.wait_recv()
+        done.wait_send()
+        s1s[g] = (acc[g] + s0r[g].astype(F32)).astype(BF)
+        for j in z_order:
+            rows = lax.rem(cz + j, chips_z) * chunk
+            for i in range(1, chips_x):
+                px = lax.rem(cx + i, chips_x)
+                remote(
+                    s1s.at[g, pl.ds(px * piece + rows, chunk)],
+                    s1r.at[g, j, cx],
+                    gsem.at[g, 1],
+                    xr_sem.at[g, j],
+                    dom=dom_of(px, cz),
+                ).start()
+
+    def z_start(g):
+        for j in z_order:
+            pz = lax.rem(cz + j, chips_z)
+            some = s1r.at[g, j, pl.ds(0, chips_x - 1)]
+            remote(some, some, gsem.at[g, 1], xr_sem.at[g, j], dom=sibling).wait_recv()
+            mine = pl.ds(cx * piece + pz * chunk, chunk)
+            total = acc[g, mine] + s0r[g, mine].astype(F32)
+            for i in range(1, chips_x):
+                total += s1r[g, j, lax.rem(cx + i, chips_x)].astype(F32)
+            if j == 0:
+                acc[g, mine] = total
+                continue
+            s2s[g, j] = total.astype(BF)
+            remote(
+                s2s.at[g, j], s2r.at[g, cz], gsem.at[g, 2], zr_sem.at[g], dom=dom_of(cx, pz)
+            ).start()
+
+    def chunk_at(g, x, z):
+        return gout.at[g, core, pl.ds(x * piece + z * chunk, chunk)]
+
+    def finish(g):
+        some = s2r.at[g, pl.ds(0, chips_z - 1)]
+        remote(some, some, gsem.at[g, 2], zr_sem.at[g], dom=sibling).wait_recv()
+        total = acc[g, pl.ds(cx * piece + cz * chunk, chunk)]
+        for i in range(1, chips_z):
+            total += s2r[g, lax.rem(cz + i, chips_z)].astype(F32)
+        fin[g] = (total * factor).astype(BF)
+        place = chunk_at(g, cx, cz)
+        for j in z_order:
+            if j:
+                pz = lax.rem(cz + j, chips_z)
+                remote(fin.at[g], place, gsem.at[g, 3], za_sem.at[g, j], dom=dom_of(cx, pz)).start()
+        for i in range(1, chips_x):
+            px = lax.rem(cx + i, chips_x)
+            remote(fin.at[g], place, gsem.at[g, 4], xa_sem.at[g], dom=dom_of(px, cz)).start()
+        pltpu.make_async_copy(fin.at[g], place, lsem.at[5 + g]).start()
+
+    def forward(g):
+        for j in reversed(z_order):
+            if j:
+                place = chunk_at(g, cx, lax.rem(cz + chips_z - j, chips_z))
+                remote(place, place, gsem.at[g, 3], za_sem.at[g, j], dom=sibling).wait_recv()
+                for i in range(1, chips_x):
+                    px = lax.rem(cx + i, chips_x)
+                    remote(place, place, gsem.at[g, 4], xa_sem.at[g], dom=dom_of(px, cz)).start()
+
+    def core_back(g):
+        place = chunk_at(g, cx, cz)
+        pltpu.make_async_copy(fin.at[g], place, lsem.at[5 + g]).wait()
+        some = gout.at[g, core, pl.ds(0, (chips_x - 1) * piece)]
+        remote(some, some, gsem.at[g, 4], xa_sem.at[g], dom=sibling).wait_recv()
+        mine = gout.at[g, core]
+        remote(mine, mine, gsem.at[g, 5], ca_sem.at[g], dom=sibling).start()
+
+    def drain(g):
+        def sent(stage, ref):
+            remote(ref, ref, gsem.at[g, stage], ca_sem.at[g], dom=sibling).wait_send()
+
+        most = (chips_x - 1) * piece
+        sent(1, s1s.at[g, pl.ds(0, most)])
+        sent(2, s2s.at[g, pl.ds(0, chips_z - 1)])
+        sent(3, s2s.at[g, pl.ds(0, chips_z - 1)])
+        sent(4, s1s.at[g, pl.ds(0, most)])
+        mine = gout.at[g, core]
+        done = remote(mine, mine, gsem.at[g, 5], ca_sem.at[g], dom=sibling)
+        done.wait_recv()
+        done.wait_send()
 
     for h in range(hids):
         s0s[0, block(h)] = dot_t(left[1 - core, h], back_pre).astype(BF)
     to_sibling(0).start()
     for h in range(hids):
         acc[0, block(h)] = dot_t(left[core, h], back_pre)
+    x_start(0)
 
     gather_wait(3, hid_all, hid_all)
     mixed = dot(hid_all[0], w_v[3, block(0)])
     for h in range(1, hids):
         mixed += dot(hid_all[h], w_v[3, block(h)])
     mixed = mixed.astype(BF)
-    send3[...] = pack(dot(onehot[...], mixed), slots)
-    exchange_start(2, send3, recv3)
+    send[4] = pack(dot(onehot[...], mixed), slots)
+    exchange_start(4)
 
     for h in range(hids):
         s0s[1, block(h)] = dot_t(hid_all[h], right[1 - core]).astype(BF)
     to_sibling(1).start()
     for h in range(hids):
         acc[1, block(h)] = dot_t(hid_all[h], right[core])
-
-    def dom_of(x, z):
-        return (x * chips_z + z) * 2 + core
-
-    def x_start(g):
-        done = to_sibling(g)
-        done.wait_recv()
-        done.wait_send()
-        s1s[g] = (acc[g] + s0r[g].astype(F32)).astype(BF)
-        mine = pl.ds(cx * piece, piece)
-        own1[g] = acc[g, mine] + s0r[g, mine].astype(F32)
-        for i in range(1, chips_x):
-            px = lax.rem(cx + i, chips_x)
-            remote(
-                s1s.at[g, pl.ds(px * piece, piece)],
-                s1r.at[g, cx],
-                gsem.at[g, 1],
-                grsem.at[g, 1],
-                dom=dom_of(px, cz),
-            ).start()
-
-    def z_start(g):
-        some = pl.ds(0, (chips_x - 1) * piece)
-        done = remote(
-            s1s.at[g, some], s1s.at[g, some], gsem.at[g, 1], grsem.at[g, 1], dom=sibling
-        )
-        done.wait_recv()
-        done.wait_send()
-        total = own1[g]
-        for i in range(1, chips_x):
-            total += s1r[g, lax.rem(cx + i, chips_x)].astype(F32)
-        own1[g] = total
-        s2s[g] = total.astype(BF)
-        for i in range(1, chips_z):
-            pz = lax.rem(cz + i, chips_z)
-            remote(
-                s2s.at[g, pl.ds(pz * chunk, chunk)],
-                s2r.at[g, cz],
-                gsem.at[g, 2],
-                grsem.at[g, 2],
-                dom=dom_of(cx, pz),
-            ).start()
-
-    def z_back(g):
-        some = pl.ds(0, (chips_z - 1) * chunk)
-        done = remote(
-            s2s.at[g, some], s2s.at[g, some], gsem.at[g, 2], grsem.at[g, 2], dom=sibling
-        )
-        done.wait_recv()
-        done.wait_send()
-        total = own1[g, pl.ds(cz * chunk, chunk)]
-        for i in range(1, chips_z):
-            total += s2r[g, lax.rem(cz + i, chips_z)].astype(F32)
-        fin[g] = (total * factor).astype(BF)
-        place = gout.at[g, core, pl.ds(cx * piece + cz * chunk, chunk)]
-        pltpu.make_async_copy(fin.at[g], place, lsem.at[5 + g]).start()
-        for i in range(1, chips_z):
-            pz = lax.rem(cz + i, chips_z)
-            remote(fin.at[g], place, gsem.at[g, 3], grsem.at[g, 3], dom=dom_of(cx, pz)).start()
-
-    def x_back(g):
-        place = gout.at[g, core, pl.ds(cx * piece + cz * chunk, chunk)]
-        pltpu.make_async_copy(fin.at[g], place, lsem.at[5 + g]).wait()
-        some = gout.at[g, core, pl.ds(0, (chips_z - 1) * chunk)]
-        done = remote(some, some, gsem.at[g, 3], grsem.at[g, 3], dom=sibling)
-        done.wait_recv()
-        done.wait_send()
-        mine = gout.at[g, core, pl.ds(cx * piece, piece)]
-        for i in range(1, chips_x):
-            px = lax.rem(cx + i, chips_x)
-            remote(mine, mine, gsem.at[g, 4], grsem.at[g, 4], dom=dom_of(px, cz)).start()
-
-    def core_back(g):
-        some = gout.at[g, core, pl.ds(0, (chips_x - 1) * piece)]
-        done = remote(some, some, gsem.at[g, 4], grsem.at[g, 4], dom=sibling)
-        done.wait_recv()
-        done.wait_send()
-        mine = gout.at[g, core]
-        remote(mine, mine, gsem.at[g, 5], grsem.at[g, 5], dom=sibling).start()
-
-    x_start(0)
-
-    exchange_wait(2, send3, recv3)
-    held = unpack(recv3[...], slots)
-    send4[...] = pack(dot(adj[low, top], mixed) + dot(adj[low, low], held), slots)
-    exchange_start(3, send4, recv4)
     x_start(1)
+    z_start(0)
+    finish(0)
+
+    held = exchange_wait(4)
+    send[5] = pack(dot(adj[low, top], mixed) + dot(adj[low, low], held), slots)
+    exchange_start(5)
+    z_start(1)
+    forward(0)
     total = dot(adj[top, top], mixed) + dot(adj[top, low], held)
     for h in range(hids):
         total += dot(hid_all[h], w_v[1, block(h)])
     own_v[0] = total
-
-    z_start(0)
-    z_back(0)
-    exchange_wait(3, send4, recv4)
-    out[...] = (own_v[0] + dot(onehot_t[...], unpack(recv4[...], slots))).astype(BF)
-    z_start(1)
-    x_back(0)
-    z_back(1)
+    finish(1)
     core_back(0)
-    x_back(1)
+    forward(1)
+    out[...] = (own_v[0] + dot(onehot_t[...], exchange_wait(5))).astype(BF)
     core_back(1)
-    for g in range(2):
-        mine = gout.at[g, core]
-        done = remote(mine, mine, gsem.at[g, 5], grsem.at[g, 5], dom=sibling)
-        done.wait_recv()
-        done.wait_send()
+    drain(0)
+    drain(1)
 
 
 def local(
@@ -453,10 +450,8 @@
             pltpu.VMEM((masters, mirrors), BF),
             pltpu.VMEM((side, side), BF),
             pltpu.VMEM((side, side), BF),
-        ]
-        + [pltpu.VMEM((doms, 2 * packed, LANES), BF)] * 4
-        + [pltpu.VMEM((doms, packed, LANES), BF)] * 4
-        + [
+            pltpu.VMEM((6, doms, packed, LANES), BF),
+            pltpu.VMEM((6, doms, packed, LANES), BF),
             pltpu.VMEM((2, hids, masters, narrow), BF),
             pltpu.VMEM((hids, masters, narrow), BF),
             pltpu.VMEM((2, masters, narrow), BF),
@@ -469,21 +464,25 @@
             pltpu.VMEM((2, width, narrow), BF),
             pltpu.VMEM((2, width, narrow), BF),
             pltpu.VMEM((2, width, narrow), BF),
-            pltpu.VMEM((2, chips_x, piece, narrow), BF),
-            pltpu.VMEM((2, piece, narrow), F32),
-            pltpu.VMEM((2, piece, narrow), BF),
+            pltpu.VMEM((2, CHIPS_Z, chips_x, chunk, narrow), BF),
+            pltpu.VMEM((2, CHIPS_Z, chunk, narrow), BF),
             pltpu.VMEM((2, CHIPS_Z, chunk, narrow), BF),
             pltpu.VMEM((2, chunk, narrow), BF),
             dma((7,)),
-            dma((4,)),
-            dma((4,)),
+            dma((6,)),
+            dma((6,)),
             dma((4,)),
             dma((4,)),
             dma((2, 6)),
-            dma((2, 6)),
+            dma((2,)),
+            dma((2, CHIPS_Z)),
+            dma((2,)),
+            dma((2, CHIPS_Z)),
+            dma((2,)),
+            dma((2,)),
         ],
         compiler_params=pltpu.CompilerParams(
-            collective_id=0, has_side_effects=True, vmem_limit_bytes=48 * 1024 * 1024
+            collective_id=0, has_side_effects=True, vmem_limit_bytes=60 * 1024 * 1024
         ),
     )(
         slot_of,

time: 123 us -> 101 us (0.82)
  Pallas kernels: 109 us -> 93.5 us
  local copies, waits for them, and re-layouts: 11.3 us -> 2.74 us
  other arithmetic: 1.12 us -> 3.22 us
    pallas_call x1, Pallas kernels: 109 us -> 93.5 us  [local(): pl.pallas_call(body, out_shape=(jax.ShapeDtypeStruct((masters, narrow), B...]
    unnamed x19 -> x3, local copies, waits for them, and re-layouts: 9.18 us -> 0.66 us
    convert_element_type x1, other arithmetic: 0.36 us -> 1.95 us  [local(): grads = grads.astype(F32)]
where the time goes in v2:
time: 101 us
  Pallas kernels  93.5 us (93%)
  other arithmetic  3.22 us (3%)
  local copies, waits for them, and re-layouts  2.74 us (3%)
  between operations  1.31 us (1%)
    pallas_call x1, Pallas kernels, local(): pl.pallas_call(body, out_shape=(jax.ShapeDtypeStruct((masters, narrow), B...  93.5 us
    squeeze x1, local copies, waits for them, and re-layouts, local(): return (out, grads[0, 0], grads[0, 1], grads[1, 0], grads[1, 1])  2.08 us

profile of v2, /device:TPU:1, one launch (start us, length us, event | category | flops | bytes accessed | tf_op | source)
XLA Modules:
  0.0 100.7 jit_solution(13697603477755759044)
XLA Ops:
  1.3 1.3 %convert_reduce_fusion = (s32[36]{0:T(128)}, s32[36]{0:T(128)}) fusion(s32[32]{0:T(128)} %bitcast.13, pred[32]{0:T(512)(128)(4,1)S(1)} %iota_compare_fusion.1), kind=kLoop, calls=%fused_computation.4 | loop fusion | flops 6840 | bytes 448 | tf_op jit(solution)/shard_map/reduce_sum | solution.py:427
  2.6 93.5 %shard_map.146 = (bf16[256,256]{1,0:T(8,128)(2,1)}, bf16[2,2,1024,256]{3,2,1,0:T(8,128)(2,1)}) custom-call(s32[36]{0:T(128)} %get-tuple-element.10.refs_0_, s32[36]{0:T(128)} %get-tuple-element.9.refs_1_, bf16[256,256]{1,0:T(8,128)(2,1)} %refs_2_.1, bf16[256,256]{1,0:T(8,128)(2,1)} %refs_3_.1, s32[1,512]{1,0:T(1,128)} %refs_4_.1, s32[1,64]{1,0:T(1,128)} %refs_5_.1, ...), custom_call_target="tpu_custom_call" | custom-call | tf_op jit(solution)/shard_map/pallas_call | solution.py:438
  96.0 2.0 %convert_element_type.7 = f32[2,2,1024,256]{3,2,1,0:T(8,128)S(1)} convert(bf16[2,2,1024,256]{3,2,1,0:T(8,128)(2,1)} %get-tuple-element.8) | non-fusion elementwise | flops 1048576 | bytes 6291456 | tf_op jit(solution)/shard_map/convert_element_type | solution.py:500
  98.0 0.0 copy-start
  98.0 2.1 %slice_bitcast_fusion = (f32[1024,256]{1,0:T(8,128)}, f32[1024,256]{1,0:T(8,128)}, f32[1024,256]{1,0:T(8,128)}, f32[1024,256]{1,0:T(8,128)}) fusion(f32[2,2,1024,256]{3,2,1,0:T(8,128)S(1)} %convert_element_type.7), kind=kLoop, calls=%fused_computation | loop fusion | bytes 8388608 | tf_op jit(solution)/shard_map/squeeze | solution.py:501
  100.1 0.0 copy-done
  100.1 0.7 copy.18
  (1 shorter events, 0.0 us)
Async XLA Ops:
  98.0 2.1 %copy-start = (bf16[256,256]{1,0:T(8,128)(2,1)S(1)}, bf16[256,256]{1,0:T(8,128)(2,1)}, u32[]{:S(2)}) copy-start(bf16[256,256]{1,0:T(8,128)(2,1)} %get-tuple-element.20) | copy-start | bytes 393220

commit v3 on v2

--- a/solution.py
+++ b/solution.py
@@ -45,8 +45,8 @@
 
 def kernel(
     dims,
-    slot_of,
-    used,
+    tile_at,
+    tile_total,
     feat,
     cot,
     slot_row,
@@ -69,7 +69,6 @@
     left,
     hid_all,
     right,
-    back_f32,
     rs_send,
     rs_recv,
     pre_v,
@@ -141,8 +140,8 @@
     loads = [pltpu.make_async_copy(tiles, tiles_v, lsem.at[0])]
     for i, w in enumerate((ws1, ws2, wn1, wn2)):
         loads.append(pltpu.make_async_copy(w, w_v.at[i], lsem.at[i + 1]))
-    for load in loads:
-        load.start()
+    for i in (4, 0, 2, 1, 3):
+        loads[i].start()
 
     grp = lax.broadcasted_iota(I32, (doms, mirrors), 0)
     col = lax.broadcasted_iota(I32, (doms, mirrors), 1)
@@ -157,11 +156,8 @@
     onehot[...] = hot.T.astype(BF)
 
     send[0] = pack(dot(onehot[...], feat[...]), slots)
-    send[1] = pack(dot(onehot[...], cot[...]), slots)
     for n in range(recv.shape[0]):
         recv[n, me] = jnp.zeros(recv.shape[2:], BF)
-    left[0, hid] = feat[...]
-    right[0] = cot[...]
 
     pl.semaphore_wait(barrier, doms - 1 + hids - 1)
 
@@ -192,27 +188,52 @@
         done.wait_recv()
         done.wait_send()
 
+    def scatter_start(n):
+        for i in range(1, hids):
+            peer = lax.rem(hid + i, hids)
+            remote(
+                rs_send.at[n, peer], rs_recv.at[n, hid], ysem.at[2 + n], yrsem.at[2 + n], hid=peer
+            ).start()
+
+    def scatter_wait(n):
+        gather_wait(2 + n, rs_send.at[n], rs_recv.at[n])
+        total = rs_send[n, hid].astype(F32)
+        for i in range(1, hids):
+            total += rs_recv[n, lax.rem(hid + i, hids)].astype(F32)
+        return total
+
+    def block(h):
+        return pl.ds(h * narrow, narrow)
+
     exchange_start(0)
+    loads[4].wait()
+    for h in range(hids):
+        rs_send[0, h] = dot_r(cot[...], w_v[3, block(h)]).astype(BF)
+    scatter_start(0)
     gather_start(0, feat, left.at[0, hid])
+    send[1] = pack(dot(onehot[...], cot[...]), slots)
     exchange_start(1)
+    left[0, hid] = feat[...]
+    right[0] = cot[...]
 
     loads[0].wait()
+    total_tiles = tile_total[0]
     for r in range(blocks):
         for c in range(blocks):
             e = r * blocks + c
-            tile = jnp.where(used[e] > 0, tiles_v[slot_of[e]], jnp.zeros((), BF))
+            found = jnp.int32(0)
+            for t in range(tiles.shape[0]):
+                hit = jnp.logical_and(tile_at[0, t] == e, t < total_tiles)
+                found = jnp.where(hit, t + 1, found)
+            tile = jnp.where(found > 0, tiles_v[jnp.maximum(found - 1, 0)], jnp.zeros((), BF))
             rs, cs = pl.ds(r * size, size), pl.ds(c * size, size)
             adj[rs, cs] = tile
             adj_t[cs, rs] = tile.astype(F32).T.astype(BF)
 
-    for load in loads[1:]:
-        load.wait()
-
-    def block(h):
-        return pl.ds(h * narrow, narrow)
-
-    for h in range(hids):
-        back_f32[h] = dot_r(cot[...], w_v[1, block(h)])
+    loads[2].wait()
+    for h in range(hids):
+        rs_send[1, h] = dot_r(cot[...], w_v[1, block(h)]).astype(BF)
+    scatter_start(1)
 
     top, low = pl.ds(0, masters), pl.ds(masters, mirrors)
     held = exchange_wait(0)
@@ -220,12 +241,17 @@
     exchange_start(2)
     own_v[0] = dot(adj[top, top], feat[...]) + dot(adj[top, low], held)
 
+    back_agg = scatter_wait(0).astype(BF)
+    send[3] = pack(dot(onehot[...], back_agg), slots)
+    exchange_start(3)
+
     held = exchange_wait(1)
-    send[3] = pack(dot(adj_t[low, top], cot[...]) + dot(adj_t[low, low], held), slots)
-    exchange_start(3)
+    send[5] = pack(dot(adj_t[low, top], cot[...]) + dot(adj_t[low, low], held), slots)
     own_v[1] = dot(adj_t[top, top], cot[...]) + dot(adj_t[top, low], held)
 
     gather_wait(0, left.at[0], left.at[0])
+    loads[1].wait()
+    loads[3].wait()
     pre = dot(left[0, 0], w_v[0, block(0)])
     for h in range(1, hids):
         pre += dot(left[0, h], w_v[0, block(h)])
@@ -233,12 +259,14 @@
 
     left[1, hid] = (own_v[0] + dot(onehot_t[...], exchange_wait(2))).astype(BF)
     gather_start(1, left.at[1, hid], left.at[1, hid])
-    right[1] = (own_v[1] + dot(onehot_t[...], exchange_wait(3))).astype(BF)
-    for h in range(hids):
-        rs_send[h] = (back_f32[h] + dot_r(right[1], w_v[3, block(h)])).astype(BF)
-    for i in range(1, hids):
-        peer = lax.rem(hid + i, hids)
-        remote(rs_send.at[peer], rs_recv.at[hid], ysem.at[2], yrsem.at[2], hid=peer).start()
+
+    held = exchange_wait(3)
+    send[4] = pack(dot(adj_t[low, top], back_agg) + dot(adj_t[low, low], held), slots)
+    exchange_start(4)
+    exchange_start(5)
+    own_v[0] = (
+        dot(adj_t[top, top], back_agg) + dot(adj_t[top, low], held) + scatter_wait(1)
+    )
 
     gather_wait(1, left.at[1], left.at[1])
     pre = pre_v[...]
@@ -246,12 +274,9 @@
         pre += dot(left[1, h], w_v[2, block(h)])
     sigma = jax.nn.sigmoid(pre)
     hid_all[hid] = (pre * sigma).astype(BF)
-    gather_start(3, hid_all.at[hid], hid_all.at[hid])
-
-    gather_wait(2, rs_send, rs_recv)
-    back_one = rs_send[hid].astype(F32)
-    for i in range(1, hids):
-        back_one += rs_recv[lax.rem(hid + i, hids)].astype(F32)
+    gather_start(4, hid_all.at[hid], hid_all.at[hid])
+
+    back_one = own_v[0] + dot(onehot_t[...], exchange_wait(4))
     back_pre = (back_one * sigma * (1.0 + pre * (1.0 - sigma))).astype(BF)
 
     sibling = me + 1 - 2 * core
@@ -358,13 +383,14 @@
         acc[0, block(h)] = dot_t(left[core, h], back_pre)
     x_start(0)
 
-    gather_wait(3, hid_all, hid_all)
+    right[1] = (own_v[1] + dot(onehot_t[...], exchange_wait(5))).astype(BF)
+    gather_wait(4, hid_all, hid_all)
     mixed = dot(hid_all[0], w_v[3, block(0)])
     for h in range(1, hids):
         mixed += dot(hid_all[h], w_v[3, block(h)])
     mixed = mixed.astype(BF)
-    send[4] = pack(dot(onehot[...], mixed), slots)
-    exchange_start(4)
+    send[6] = pack(dot(onehot[...], mixed), slots)
+    exchange_start(6)
 
     for h in range(hids):
         s0s[1, block(h)] = dot_t(hid_all[h], right[1 - core]).astype(BF)
@@ -375,9 +401,9 @@
     z_start(0)
     finish(0)
 
-    held = exchange_wait(4)
-    send[5] = pack(dot(adj[low, top], mixed) + dot(adj[low, low], held), slots)
-    exchange_start(5)
+    held = exchange_wait(6)
+    send[7] = pack(dot(adj[low, top], mixed) + dot(adj[low, low], held), slots)
+    exchange_start(7)
     z_start(1)
     forward(0)
     total = dot(adj[top, top], mixed) + dot(adj[top, low], held)
@@ -387,7 +413,7 @@
     finish(1)
     core_back(0)
     forward(1)
-    out[...] = (own_v[0] + dot(onehot_t[...], exchange_wait(5))).astype(BF)
+    out[...] = (own_v[0] + dot(onehot_t[...], exchange_wait(7))).astype(BF)
     core_back(1)
     drain(0)
     drain(1)
@@ -418,14 +444,6 @@
     piece = width // chips_x
     chunk = piece // CHIPS_Z
 
-    order = jnp.arange(tiles.shape[1], dtype=I32)
-    match = (
-        (tile_index[0][None, :] == jnp.arange(blocks * blocks, dtype=I32)[:, None])
-        & (order < tile_count[0])[None, :]
-    ).astype(I32)
-    slot_of = (match * order[None, :]).sum(axis=1)
-    used = match.sum(axis=1)
-
     packed = slots * narrow // LANES
     smem = pl.BlockSpec(memory_space=pltpu.SMEM)
     vmem = pl.BlockSpec(memory_space=pltpu.VMEM)
@@ -450,14 +468,13 @@
             pltpu.VMEM((masters, mirrors), BF),
             pltpu.VMEM((side, side), BF),
             pltpu.VMEM((side, side), BF),
-            pltpu.VMEM((6, doms, packed, LANES), BF),
-            pltpu.VMEM((6, doms, packed, LANES), BF),
+            pltpu.VMEM((8, doms, packed, LANES), BF),
+            pltpu.VMEM((8, doms, packed, LANES), BF),
             pltpu.VMEM((2, hids, masters, narrow), BF),
             pltpu.VMEM((hids, masters, narrow), BF),
             pltpu.VMEM((2, masters, narrow), BF),
-            pltpu.VMEM((hids, masters, narrow), F32),
-            pltpu.VMEM((hids, masters, narrow), BF),
-            pltpu.VMEM((hids, masters, narrow), BF),
+            pltpu.VMEM((2, hids, masters, narrow), BF),
+            pltpu.VMEM((2, hids, masters, narrow), BF),
             pltpu.VMEM((masters, narrow), F32),
             pltpu.VMEM((2, masters, narrow), F32),
             pltpu.VMEM((2, width, narrow), F32),
@@ -469,10 +486,10 @@
             pltpu.VMEM((2, CHIPS_Z, chunk, narrow), BF),
             pltpu.VMEM((2, chunk, narrow), BF),
             dma((7,)),
-            dma((6,)),
-            dma((6,)),
-            dma((4,)),
-            dma((4,)),
+            dma((8,)),
+            dma((8,)),
+            dma((5,)),
+            dma((5,)),
             dma((2, 6)),
             dma((2,)),
             dma((2, CHIPS_Z)),
@@ -485,8 +502,8 @@
             collective_id=0, has_side_effects=True, vmem_limit_bytes=60 * 1024 * 1024
         ),
     )(
-        slot_of,
-        used,
+        tile_index,
+        tile_count,
         feat,
         cotangent,
         replica_slot,
@@ -497,8 +514,7 @@
         w_self2,
         w_neigh2,
     )
-    grads = grads.astype(F32)
-    return (out, grads[0, 0], grads[0, 1], grads[1, 0], grads[1, 1])
+    return (out, *(grads[i // 2, i % 2].astype(F32) for i in range(4)))
 
 
 def solution(mesh):

time: 101 us -> 100 us (0.990)
  local copies, waits for them, and re-layouts: 2.74 us -> 0.66 us
    squeeze x1 -> x0, local copies, waits for them, and re-layouts: 2.08 us -> none  [local(): return (out, grads[0, 0], grads[0, 1], grads[1, 0], grads[1, 1])]
    convert_element_type x1, other arithmetic: 1.95 us -> 3.64 us  [local(): return (out, *(grads[i // 2, i % 2].astype(F32) for i in range(4)))]
    reduce_sum x1 -> x0, other arithmetic: 1.26 us -> none  [local(): used = match.sum(axis=1)]
where the time goes in v3:
time: 100 us
  Pallas kernels  94.4 us (94%)
  other arithmetic  3.64 us (4%)
  between operations  1.3 us (1%)
    pallas_call x1, Pallas kernels, local(): pl.pallas_call(body, out_shape=(jax.ShapeDtypeStruct((masters, narrow), B...  94.4 us
    convert_element_type x1, other arithmetic, local(): return (out, *(grads[i // 2, i % 2].astype(F32) for i in range(4)))  3.64 us

profile of v3, /device:TPU:1, one launch (start us, length us, event | category | flops | bytes accessed | tf_op | source)
XLA Modules:
  0.0 100.0 jit_solution(16742234124769492801)
XLA Ops:
  1.3 94.4 %shard_map.146 = (bf16[256,256]{1,0:T(8,128)(2,1)}, bf16[2,2,1024,256]{3,2,1,0:T(8,128)(2,1)}) custom-call(s32[1,32]{1,0:T(1,128)} %refs_0_.1, s32[1]{0:T(128)S(6)} %copy.17.refs_1_, bf16[256,256]{1,0:T(8,128)(2,1)} %refs_2_.1, bf16[256,256]{1,0:T(8,128)(2,1)} %refs_3_.1, s32[1,512]{1,0:T(1,128)} %refs_4_.1, s32[1,64]{1,0:T(1,128)} %refs_5_.1, ...), custom_call_target="tpu_custom_call" | custom-call | tf_op jit(solution)/shard_map/pallas_call | solution.py:456
  95.7 0.0 copy-start
  95.7 3.6 %bitcast_convert_fusion = (f32[1024,256]{1,0:T(8,128)}, f32[1024,256]{1,0:T(8,128)}, f32[1024,256]{1,0:T(8,128)}, f32[1024,256]{1,0:T(8,128)}) fusion(bf16[2,2,1024,256]{3,2,1,0:T(8,128)(2,1)} %get-tuple-element.8), kind=kLoop, calls=%fused_computation | loop fusion | flops 1048576 | bytes 6291456 | tf_op jit(solution)/shard_map/convert_element_type | solution.py:517
  99.4 0.0 copy-done
  99.4 0.7 copy.18
Async XLA Ops:
  95.7 3.6 %copy-start = (bf16[256,256]{1,0:T(8,128)(2,1)S(1)}, bf16[256,256]{1,0:T(8,128)(2,1)}, u32[]{:S(2)}) copy-start(bf16[256,256]{1,0:T(8,128)(2,1)} %get-tuple-element.18) | copy-start | bytes 393220

commit v4 on v2

--- a/solution.py
+++ b/solution.py
@@ -45,8 +45,8 @@
 
 def kernel(
     dims,
-    slot_of,
-    used,
+    tile_at,
+    tile_total,
     feat,
     cot,
     slot_row,
@@ -68,6 +68,7 @@
     recv,
     left,
     hid_all,
+    agg_two,
     right,
     back_f32,
     rs_send,
@@ -138,9 +139,21 @@
             device_id_type=pl.DeviceIdType.MESH,
         )
 
-    loads = [pltpu.make_async_copy(tiles, tiles_v, lsem.at[0])]
-    for i, w in enumerate((ws1, ws2, wn1, wn2)):
-        loads.append(pltpu.make_async_copy(w, w_v.at[i], lsem.at[i + 1]))
+    mine_in = left.at[0, hid]
+    loads = [
+        pltpu.make_async_copy(src, dst, lsem.at[i])
+        for i, (src, dst) in enumerate(
+            (
+                (feat, mine_in),
+                (cot, right.at[0]),
+                (tiles, tiles_v),
+                (ws2, w_v.at[1]),
+                (ws1, w_v.at[0]),
+                (wn1, w_v.at[2]),
+                (wn2, w_v.at[3]),
+            )
+        )
+    ]
     for load in loads:
         load.start()
 
@@ -156,12 +169,10 @@
     onehot_t[...] = hot.astype(BF)
     onehot[...] = hot.T.astype(BF)
 
-    send[0] = pack(dot(onehot[...], feat[...]), slots)
-    send[1] = pack(dot(onehot[...], cot[...]), slots)
+    loads[0].wait()
+    send[0] = pack(dot(onehot[...], mine_in[...]), slots)
     for n in range(recv.shape[0]):
         recv[n, me] = jnp.zeros(recv.shape[2:], BF)
-    left[0, hid] = feat[...]
-    right[0] = cot[...]
 
     pl.semaphore_wait(barrier, doms - 1 + hids - 1)
 
@@ -193,37 +204,44 @@
         done.wait_send()
 
     exchange_start(0)
-    gather_start(0, feat, left.at[0, hid])
+    loads[1].wait()
+    send[1] = pack(dot(onehot[...], right[0]), slots)
     exchange_start(1)
-
-    loads[0].wait()
+    gather_start(0, mine_in, mine_in)
+
+    loads[2].wait()
+    total_tiles = tile_total[0]
     for r in range(blocks):
         for c in range(blocks):
             e = r * blocks + c
-            tile = jnp.where(used[e] > 0, tiles_v[slot_of[e]], jnp.zeros((), BF))
+            found = jnp.int32(0)
+            for t in range(tiles.shape[0]):
+                hit = jnp.logical_and(tile_at[0, t] == e, t < total_tiles)
+                found = jnp.where(hit, t + 1, found)
+            tile = jnp.where(found > 0, tiles_v[jnp.maximum(found - 1, 0)], jnp.zeros((), BF))
             rs, cs = pl.ds(r * size, size), pl.ds(c * size, size)
             adj[rs, cs] = tile
             adj_t[cs, rs] = tile.astype(F32).T.astype(BF)
 
-    for load in loads[1:]:
+    for load in loads[3:]:
         load.wait()
 
     def block(h):
         return pl.ds(h * narrow, narrow)
 
     for h in range(hids):
-        back_f32[h] = dot_r(cot[...], w_v[1, block(h)])
+        back_f32[h] = dot_r(right[0], w_v[1, block(h)])
 
     top, low = pl.ds(0, masters), pl.ds(masters, mirrors)
     held = exchange_wait(0)
-    send[2] = pack(dot(adj[low, top], feat[...]) + dot(adj[low, low], held), slots)
+    send[2] = pack(dot(adj[low, top], mine_in[...]) + dot(adj[low, low], held), slots)
     exchange_start(2)
-    own_v[0] = dot(adj[top, top], feat[...]) + dot(adj[top, low], held)
+    own_v[0] = dot(adj[top, top], mine_in[...]) + dot(adj[top, low], held)
 
     held = exchange_wait(1)
-    send[3] = pack(dot(adj_t[low, top], cot[...]) + dot(adj_t[low, low], held), slots)
+    send[3] = pack(dot(adj_t[low, top], right[0]) + dot(adj_t[low, low], held), slots)
     exchange_start(3)
-    own_v[1] = dot(adj_t[top, top], cot[...]) + dot(adj_t[top, low], held)
+    own_v[1] = dot(adj_t[top, top], right[0]) + dot(adj_t[top, low], held)
 
     gather_wait(0, left.at[0], left.at[0])
     pre = dot(left[0, 0], w_v[0, block(0)])
@@ -247,6 +265,8 @@
     sigma = jax.nn.sigmoid(pre)
     hid_all[hid] = (pre * sigma).astype(BF)
     gather_start(3, hid_all.at[hid], hid_all.at[hid])
+    send[4] = pack(dot(onehot[...], hid_all[hid]), slots)
+    exchange_start(4)
 
     gather_wait(2, rs_send, rs_recv)
     back_one = rs_send[hid].astype(F32)
@@ -318,7 +338,7 @@
         for i in range(1, chips_x):
             px = lax.rem(cx + i, chips_x)
             remote(fin.at[g], place, gsem.at[g, 4], xa_sem.at[g], dom=dom_of(px, cz)).start()
-        pltpu.make_async_copy(fin.at[g], place, lsem.at[5 + g]).start()
+        pltpu.make_async_copy(fin.at[g], place, lsem.at[7 + g]).start()
 
     def forward(g):
         for j in reversed(z_order):
@@ -331,7 +351,7 @@
 
     def core_back(g):
         place = chunk_at(g, cx, cz)
-        pltpu.make_async_copy(fin.at[g], place, lsem.at[5 + g]).wait()
+        pltpu.make_async_copy(fin.at[g], place, lsem.at[7 + g]).wait()
         some = gout.at[g, core, pl.ds(0, (chips_x - 1) * piece)]
         remote(some, some, gsem.at[g, 4], xa_sem.at[g], dom=sibling).wait_recv()
         mine = gout.at[g, core]
@@ -357,15 +377,11 @@
     for h in range(hids):
         acc[0, block(h)] = dot_t(left[core, h], back_pre)
     x_start(0)
-
+    held = exchange_wait(4)
+    send[5] = pack(dot(adj[low, top], hid_all[hid]) + dot(adj[low, low], held), slots)
+    exchange_start(5)
+    own_v[0] = dot(adj[top, top], hid_all[hid]) + dot(adj[top, low], held)
     gather_wait(3, hid_all, hid_all)
-    mixed = dot(hid_all[0], w_v[3, block(0)])
-    for h in range(1, hids):
-        mixed += dot(hid_all[h], w_v[3, block(h)])
-    mixed = mixed.astype(BF)
-    send[4] = pack(dot(onehot[...], mixed), slots)
-    exchange_start(4)
-
     for h in range(hids):
         s0s[1, block(h)] = dot_t(hid_all[h], right[1 - core]).astype(BF)
     to_sibling(1).start()
@@ -374,20 +390,22 @@
     x_start(1)
     z_start(0)
     finish(0)
-
-    held = exchange_wait(4)
-    send[5] = pack(dot(adj[low, top], mixed) + dot(adj[low, low], held), slots)
-    exchange_start(5)
+    total = dot(hid_all[0], w_v[1, block(0)])
+    for h in range(1, hids):
+        total += dot(hid_all[h], w_v[1, block(h)])
+    pre_v[...] = total
     z_start(1)
     forward(0)
-    total = dot(adj[top, top], mixed) + dot(adj[top, low], held)
-    for h in range(hids):
-        total += dot(hid_all[h], w_v[1, block(h)])
-    own_v[0] = total
+    agg_two[hid] = (own_v[0] + dot(onehot_t[...], exchange_wait(5))).astype(BF)
+    gather_start(4, agg_two.at[hid], agg_two.at[hid])
     finish(1)
     core_back(0)
     forward(1)
-    out[...] = (own_v[0] + dot(onehot_t[...], exchange_wait(5))).astype(BF)
+    gather_wait(4, agg_two, agg_two)
+    total = pre_v[...]
+    for h in range(hids):
+        total += dot(agg_two[h], w_v[3, block(h)])
+    out[...] = total.astype(BF)
     core_back(1)
     drain(0)
     drain(1)
@@ -418,18 +436,11 @@
     piece = width // chips_x
     chunk = piece // CHIPS_Z
 
-    order = jnp.arange(tiles.shape[1], dtype=I32)
-    match = (
-        (tile_index[0][None, :] == jnp.arange(blocks * blocks, dtype=I32)[:, None])
-        & (order < tile_count[0])[None, :]
-    ).astype(I32)
-    slot_of = (match * order[None, :]).sum(axis=1)
-    used = match.sum(axis=1)
-
     packed = slots * narrow // LANES
     smem = pl.BlockSpec(memory_space=pltpu.SMEM)
     vmem = pl.BlockSpec(memory_space=pltpu.VMEM)
     anym = pl.BlockSpec(memory_space=pl.ANY)
+    hbm = pl.BlockSpec(memory_space=pltpu.HBM)
     dma = pltpu.SemaphoreType.DMA
 
     def body(*refs):
@@ -441,7 +452,7 @@
             jax.ShapeDtypeStruct((masters, narrow), BF),
             jax.ShapeDtypeStruct((2, 2, width, narrow), BF),
         ),
-        in_specs=[smem] * 2 + [vmem] * 4 + [anym] * 5,
+        in_specs=[smem] * 2 + [hbm] * 2 + [vmem] * 2 + [hbm] * 5,
         out_specs=(vmem, anym),
         scratch_shapes=[
             pltpu.VMEM(tiles.shape[1:], BF),
@@ -453,6 +464,7 @@
             pltpu.VMEM((6, doms, packed, LANES), BF),
             pltpu.VMEM((6, doms, packed, LANES), BF),
             pltpu.VMEM((2, hids, masters, narrow), BF),
+            pltpu.VMEM((hids, masters, narrow), BF),
             pltpu.VMEM((hids, masters, narrow), BF),
             pltpu.VMEM((2, masters, narrow), BF),
             pltpu.VMEM((hids, masters, narrow), F32),
@@ -468,11 +480,11 @@
             pltpu.VMEM((2, CHIPS_Z, chunk, narrow), BF),
             pltpu.VMEM((2, CHIPS_Z, chunk, narrow), BF),
             pltpu.VMEM((2, chunk, narrow), BF),
-            dma((7,)),
+            dma((9,)),
             dma((6,)),
             dma((6,)),
-            dma((4,)),
-            dma((4,)),
+            dma((5,)),
+            dma((5,)),
             dma((2, 6)),
             dma((2,)),
             dma((2, CHIPS_Z)),
@@ -485,8 +497,8 @@
             collective_id=0, has_side_effects=True, vmem_limit_bytes=60 * 1024 * 1024
         ),
     )(
-        slot_of,
-        used,
+        tile_index,
+        tile_count,
         feat,
         cotangent,
         replica_slot,
@@ -497,8 +509,7 @@
         w_self2,
         w_neigh2,
     )
-    grads = grads.astype(F32)
-    return (out, grads[0, 0], grads[0, 1], grads[1, 0], grads[1, 1])
+    return (out, *(grads[i // 2, i % 2].astype(F32) for i in range(4)))
 
 
 def solution(mesh):

time: 101 us -> 92.9 us (0.920)
  Pallas kernels: 93.5 us -> 87.1 us
  local copies, waits for them, and re-layouts: 2.74 us -> 0.66 us
    pallas_call x1, Pallas kernels: 93.5 us -> 87.1 us  [local(): pl.pallas_call(body, out_shape=(jax.ShapeDtypeStruct((masters, narrow), B...]
    squeeze x1 -> x0, local copies, waits for them, and re-layouts: 2.08 us -> none  [local(): return (out, grads[0, 0], grads[0, 1], grads[1, 0], grads[1, 1])]
    convert_element_type x1, other arithmetic: 1.95 us -> 3.64 us  [local(): return (out, *(grads[i // 2, i % 2].astype(F32) for i in range(4)))]
    reduce_sum x1 -> x0, other arithmetic: 1.26 us -> none  [local(): used = match.sum(axis=1)]
where the time goes in v4:
time: 92.9 us; the launch traced here: 92.7 us
  Pallas kernels  87.1 us (94%)
  other arithmetic  3.64 us (4%)
  between operations  1.3 us (1%)
    pallas_call x1, Pallas kernels, local(): pl.pallas_call(body, out_shape=(jax.ShapeDtypeStruct((masters, narrow), B...  87.1 us
    convert_element_type x1, other arithmetic, local(): return (out, *(grads[i // 2, i % 2].astype(F32) for i in range(4)))  3.64 us

profile of v4, /device:TPU:1, one launch (start us, length us, event | category | flops | bytes accessed | tf_op | source)
XLA Modules:
  0.0 92.7 jit_solution(4147459586104664964)
XLA Ops:
  1.3 87.1 %shard_map.146 = (bf16[256,256]{1,0:T(8,128)(2,1)}, bf16[2,2,1024,256]{3,2,1,0:T(8,128)(2,1)}) custom-call(s32[1,32]{1,0:T(1,128)} %refs_0_.1, s32[1]{0:T(128)S(6)} %copy.17.refs_1_, bf16[256,256]{1,0:T(8,128)(2,1)} %refs_2_.1, bf16[256,256]{1,0:T(8,128)(2,1)} %refs_3_.1, s32[1,512]{1,0:T(1,128)} %refs_4_.1, s32[1,64]{1,0:T(1,128)} %refs_5_.1, ...), custom_call_target="tpu_custom_call" | custom-call | tf_op jit(solution)/shard_map/pallas_call | solution.py:449
  88.4 0.0 copy-start
  88.4 3.6 %bitcast_convert_fusion = (f32[1024,256]{1,0:T(8,128)}, f32[1024,256]{1,0:T(8,128)}, f32[1024,256]{1,0:T(8,128)}, f32[1024,256]{1,0:T(8,128)}) fusion(bf16[2,2,1024,256]{3,2,1,0:T(8,128)(2,1)} %get-tuple-element.8), kind=kLoop, calls=%fused_computation | loop fusion | flops 1048576 | bytes 6291456 | tf_op jit(solution)/shard_map/convert_element_type | solution.py:512
  92.1 0.0 copy-done
  92.1 0.7 copy.18
Async XLA Ops:
  88.4 3.6 %copy-start = (bf16[256,256]{1,0:T(8,128)(2,1)S(1)}, bf16[256,256]{1,0:T(8,128)(2,1)}, u32[]{:S(2)}) copy-start(bf16[256,256]{1,0:T(8,128)(2,1)} %get-tuple-element.18) | copy-start | bytes 393220

commit v5 on v4

--- a/solution.py
+++ b/solution.py
@@ -24,6 +24,11 @@
 
 def dot_r(a, b):
     return lax.dot_general(a, b, (((1,), (1,)), ((), ())), preferred_element_type=F32)
+
+
+def sum_groups(width):
+    half = width // 2
+    return tuple((m, base, half, True) for m in range(2) for base in (0, half))
 
 
 def pack(rows, slots):
@@ -79,15 +84,12 @@
     s0s,
     s0r,
     s1s,
-    s1r,
-    s2s,
-    s2r,
-    fin,
     lsem,
     esem,
     ersem,
     ysem,
     yrsem,
+    csem,
     gsem,
     cr_sem,
     xr_sem,
@@ -95,6 +97,7 @@
     za_sem,
     xa_sem,
     ca_sem,
+    *bufs,
 ):
     doms, hids, slots, masters, narrow = dims
     chips_z = CHIPS_Z
@@ -182,7 +185,9 @@
             remote(send.at[n, peer], recv.at[n, me], esem.at[n], ersem.at[n], dom=peer).start()
             return carry
 
-        lax.fori_loop(1, doms, one, 0)
+        near = doms // 3
+        lax.fori_loop(near, doms, one, 0)
+        lax.fori_loop(1, near, one, 0)
 
     def exchange_wait(n):
         some = pl.ds(0, doms - 1)
@@ -275,140 +280,203 @@
     back_pre = (back_one * sigma * (1.0 + pre * (1.0 - sigma))).astype(BF)
 
     sibling = me + 1 - 2 * core
-    piece = width // chips_x
-    chunk = piece // chips_z
     factor = 1.0 / math.sqrt(doms * masters)
-    z_order = sorted(range(chips_z), key=lambda j: -min(j, chips_z - j))
-
-    def dom_of(x, z):
-        return (x * chips_z + z) * 2 + core
-
-    def to_sibling(g):
-        return remote(s0s.at[g], s0r.at[g], gsem.at[g, 0], cr_sem.at[g], dom=sibling)
-
-    def x_start(g):
-        done = to_sibling(g)
-        done.wait_recv()
-        done.wait_send()
-        s1s[g] = (acc[g] + s0r[g].astype(F32)).astype(BF)
-        for j in z_order:
-            rows = lax.rem(cz + j, chips_z) * chunk
-            for i in range(1, chips_x):
-                px = lax.rem(cx + i, chips_x)
+
+    def far_first(n):
+        return sorted(range(n), key=lambda j: -min(j, n - j))
+
+    class Sum:
+        def __init__(self, g, m, base, rows, x_first, bufs):
+            self.g, self.m, self.base, self.rows, self.x_first = g, m, base, rows, x_first
+            self.n1, self.n2 = (chips_x, chips_z) if x_first else (chips_z, chips_x)
+            self.c1, self.c2 = (cx, cz) if x_first else (cz, cx)
+            self.piece = rows // self.n1
+            self.chunk = self.piece // self.n2
+            self.order = far_first(self.n2)
+            self.r1, self.s2, self.r2, self.fin = bufs
+
+        def dom_at(self, i1, i2):
+            x, z = (i1, i2) if self.x_first else (i2, i1)
+            return (x * chips_z + z) * 2 + core
+
+        def rows_at(self, i1, i2):
+            return pl.ds(self.base + i1 * self.piece + i2 * self.chunk, self.chunk)
+
+        def other1(self, i):
+            return lax.rem(self.c1 + i, self.n1)
+
+        def other2(self, j):
+            return lax.rem(self.c2 + j, self.n2)
+
+        def place(self, i1, i2):
+            return gout.at[self.m, core, self.rows_at(i1, i2)]
+
+        def await_recv(self, sem, chunks):
+            ref = s1s.at[self.m, pl.ds(0, chunks * self.chunk)]
+            remote(ref, ref, gsem.at[self.g, 0], sem, dom=sibling).wait_recv()
+
+        def core_copy(self):
+            part = pl.ds(self.base, self.rows)
+            return remote(
+                s0s.at[self.m, part],
+                s0r.at[self.m, part],
+                csem.at[self.g],
+                cr_sem.at[self.g],
+                dom=sibling,
+            )
+
+        def first_start(self):
+            done = self.core_copy()
+            done.wait_recv()
+            done.wait_send()
+            part = pl.ds(self.base, self.rows)
+            s1s[self.m, part] = (acc[self.m, part] + s0r[self.m, part].astype(F32)).astype(BF)
+            for j in self.order:
+                for i in range(1, self.n1):
+                    remote(
+                        s1s.at[self.m, self.rows_at(self.other1(i), self.other2(j))],
+                        self.r1.at[j, self.c1],
+                        gsem.at[self.g, 0],
+                        xr_sem.at[self.g, j],
+                        dom=self.dom_at(self.other1(i), self.c2),
+                    ).start()
+
+        def second_start(self):
+            for j in self.order:
+                self.await_recv(xr_sem.at[self.g, j], self.n1 - 1)
+                part = self.rows_at(self.c1, self.other2(j))
+                total = acc[self.m, part] + s0r[self.m, part].astype(F32)
+                for i in range(1, self.n1):
+                    total += self.r1[j, self.other1(i)].astype(F32)
+                if j == 0:
+                    acc[self.m, part] = total
+                    continue
+                self.s2[j] = total.astype(BF)
                 remote(
-                    s1s.at[g, pl.ds(px * piece + rows, chunk)],
-                    s1r.at[g, j, cx],
-                    gsem.at[g, 1],
-                    xr_sem.at[g, j],
-                    dom=dom_of(px, cz),
+                    self.s2.at[j],
+                    self.r2.at[self.c2],
+                    gsem.at[self.g, 1],
+                    zr_sem.at[self.g],
+                    dom=self.dom_at(self.c1, self.other2(j)),
                 ).start()
 
-    def z_start(g):
-        for j in z_order:
-            pz = lax.rem(cz + j, chips_z)
-            some = s1r.at[g, j, pl.ds(0, chips_x - 1)]
-            remote(some, some, gsem.at[g, 1], xr_sem.at[g, j], dom=sibling).wait_recv()
-            mine = pl.ds(cx * piece + pz * chunk, chunk)
-            total = acc[g, mine] + s0r[g, mine].astype(F32)
-            for i in range(1, chips_x):
-                total += s1r[g, j, lax.rem(cx + i, chips_x)].astype(F32)
-            if j == 0:
-                acc[g, mine] = total
-                continue
-            s2s[g, j] = total.astype(BF)
-            remote(
-                s2s.at[g, j], s2r.at[g, cz], gsem.at[g, 2], zr_sem.at[g], dom=dom_of(cx, pz)
-            ).start()
-
-    def chunk_at(g, x, z):
-        return gout.at[g, core, pl.ds(x * piece + z * chunk, chunk)]
-
-    def finish(g):
-        some = s2r.at[g, pl.ds(0, chips_z - 1)]
-        remote(some, some, gsem.at[g, 2], zr_sem.at[g], dom=sibling).wait_recv()
-        total = acc[g, pl.ds(cx * piece + cz * chunk, chunk)]
-        for i in range(1, chips_z):
-            total += s2r[g, lax.rem(cz + i, chips_z)].astype(F32)
-        fin[g] = (total * factor).astype(BF)
-        place = chunk_at(g, cx, cz)
-        for j in z_order:
-            if j:
-                pz = lax.rem(cz + j, chips_z)
-                remote(fin.at[g], place, gsem.at[g, 3], za_sem.at[g, j], dom=dom_of(cx, pz)).start()
-        for i in range(1, chips_x):
-            px = lax.rem(cx + i, chips_x)
-            remote(fin.at[g], place, gsem.at[g, 4], xa_sem.at[g], dom=dom_of(px, cz)).start()
-        pltpu.make_async_copy(fin.at[g], place, lsem.at[7 + g]).start()
-
-    def forward(g):
-        for j in reversed(z_order):
-            if j:
-                place = chunk_at(g, cx, lax.rem(cz + chips_z - j, chips_z))
-                remote(place, place, gsem.at[g, 3], za_sem.at[g, j], dom=sibling).wait_recv()
-                for i in range(1, chips_x):
-                    px = lax.rem(cx + i, chips_x)
-                    remote(place, place, gsem.at[g, 4], xa_sem.at[g], dom=dom_of(px, cz)).start()
-
-    def core_back(g):
-        place = chunk_at(g, cx, cz)
-        pltpu.make_async_copy(fin.at[g], place, lsem.at[7 + g]).wait()
-        some = gout.at[g, core, pl.ds(0, (chips_x - 1) * piece)]
-        remote(some, some, gsem.at[g, 4], xa_sem.at[g], dom=sibling).wait_recv()
-        mine = gout.at[g, core]
-        remote(mine, mine, gsem.at[g, 5], ca_sem.at[g], dom=sibling).start()
-
-    def drain(g):
-        def sent(stage, ref):
-            remote(ref, ref, gsem.at[g, stage], ca_sem.at[g], dom=sibling).wait_send()
-
-        most = (chips_x - 1) * piece
-        sent(1, s1s.at[g, pl.ds(0, most)])
-        sent(2, s2s.at[g, pl.ds(0, chips_z - 1)])
-        sent(3, s2s.at[g, pl.ds(0, chips_z - 1)])
-        sent(4, s1s.at[g, pl.ds(0, most)])
-        mine = gout.at[g, core]
-        done = remote(mine, mine, gsem.at[g, 5], ca_sem.at[g], dom=sibling)
-        done.wait_recv()
-        done.wait_send()
-
-    for h in range(hids):
-        s0s[0, block(h)] = dot_t(left[1 - core, h], back_pre).astype(BF)
-    to_sibling(0).start()
+        def along_first(self, src, place):
+            for i in range(1, self.n1):
+                remote(
+                    src,
+                    place,
+                    gsem.at[self.g, 3],
+                    xa_sem.at[self.g],
+                    dom=self.dom_at(self.other1(i), self.c2),
+                ).start()
+
+        def finish(self):
+            self.await_recv(zr_sem.at[self.g], self.n2 - 1)
+            total = acc[self.m, self.rows_at(self.c1, self.c2)]
+            for j in range(1, self.n2):
+                total += self.r2[self.other2(j)].astype(F32)
+            self.fin[...] = (total * factor).astype(BF)
+            place = self.place(self.c1, self.c2)
+            for j in self.order:
+                if j:
+                    remote(
+                        self.fin,
+                        place,
+                        gsem.at[self.g, 2],
+                        za_sem.at[self.g, j],
+                        dom=self.dom_at(self.c1, self.other2(j)),
+                    ).start()
+            self.along_first(self.fin, place)
+            pltpu.make_async_copy(self.fin, place, lsem.at[7 + self.g]).start()
+
+        def forward(self):
+            for j in reversed(self.order):
+                if j:
+                    place = self.place(self.c1, lax.rem(self.c2 + self.n2 - j, self.n2))
+                    self.await_recv(za_sem.at[self.g, j], 1)
+                    self.along_first(place, place)
+
+        def sibling_copy(self):
+            mine = gout.at[self.m, core, pl.ds(self.base, self.rows)]
+            return remote(mine, mine, gsem.at[self.g, 4], ca_sem.at[self.g], dom=sibling)
+
+        def core_back(self):
+            place = self.place(self.c1, self.c2)
+            pltpu.make_async_copy(self.fin, place, lsem.at[7 + self.g]).wait()
+            self.await_recv(xa_sem.at[self.g], (self.n1 - 1) * self.n2)
+            self.sibling_copy().start()
+
+        def drain(self):
+            along1, along2 = (self.n1 - 1) * self.n2, self.n2 - 1
+            for stage, chunks in enumerate((along1, along2, along2, along1)):
+                ref = s1s.at[self.m, pl.ds(0, chunks * self.chunk)]
+                remote(ref, ref, gsem.at[self.g, stage], ca_sem.at[self.g], dom=sibling).wait_send()
+            done = self.sibling_copy()
+            done.wait_recv()
+            done.wait_send()
+
+    sums = [
+        Sum(g, *spec, bufs[4 * g : 4 * g + 4]) for g, spec in enumerate(sum_groups(width))
+    ]
+
+    early = [one for one in sums if one.m == 0]
+    late = [one for one in sums if one.m == 1]
+
+    def blocks_of(one):
+        return range(one.base // narrow, (one.base + one.rows) // narrow)
+
+    for one in early:
+        for h in blocks_of(one):
+            s0s[0, block(h)] = dot_t(left[1 - core, h], back_pre).astype(BF)
+        one.core_copy().start()
     for h in range(hids):
         acc[0, block(h)] = dot_t(left[core, h], back_pre)
-    x_start(0)
+    for one in early:
+        one.first_start()
+
     held = exchange_wait(4)
     send[5] = pack(dot(adj[low, top], hid_all[hid]) + dot(adj[low, low], held), slots)
     exchange_start(5)
     own_v[0] = dot(adj[top, top], hid_all[hid]) + dot(adj[top, low], held)
+
     gather_wait(3, hid_all, hid_all)
-    for h in range(hids):
-        s0s[1, block(h)] = dot_t(hid_all[h], right[1 - core]).astype(BF)
-    to_sibling(1).start()
+    for one in late:
+        for h in blocks_of(one):
+            s0s[1, block(h)] = dot_t(hid_all[h], right[1 - core]).astype(BF)
+        one.core_copy().start()
     for h in range(hids):
         acc[1, block(h)] = dot_t(hid_all[h], right[core])
-    x_start(1)
-    z_start(0)
-    finish(0)
+    for one in late:
+        one.first_start()
+    for one in early:
+        one.second_start()
+    for one in early:
+        one.finish()
     total = dot(hid_all[0], w_v[1, block(0)])
     for h in range(1, hids):
         total += dot(hid_all[h], w_v[1, block(h)])
     pre_v[...] = total
-    z_start(1)
-    forward(0)
+    for one in late:
+        one.second_start()
+    for one in early:
+        one.forward()
     agg_two[hid] = (own_v[0] + dot(onehot_t[...], exchange_wait(5))).astype(BF)
     gather_start(4, agg_two.at[hid], agg_two.at[hid])
-    finish(1)
-    core_back(0)
-    forward(1)
+    for one in late:
+        one.finish()
+    for one in late:
+        one.forward()
+    for one in early:
+        one.core_back()
     gather_wait(4, agg_two, agg_two)
     total = pre_v[...]
     for h in range(hids):
         total += dot(agg_two[h], w_v[3, block(h)])
     out[...] = total.astype(BF)
-    core_back(1)
-    drain(0)
-    drain(1)
+    for one in late:
+        one.core_back()
+    for one in sums:
+        one.drain()
 
 
 def local(
@@ -433,8 +501,18 @@
     blocks = (masters + mirrors) // size
     side = blocks * size
     chips_x = doms // (2 * CHIPS_Z)
-    piece = width // chips_x
-    chunk = piece // CHIPS_Z
+    groups = sum_groups(width)
+    count = len(groups)
+    buffers = []
+    for _, _, rows, x_first in groups:
+        n1, n2 = (chips_x, CHIPS_Z) if x_first else (CHIPS_Z, chips_x)
+        chunk = rows // (n1 * n2)
+        buffers += [
+            pltpu.VMEM((n2, n1, chunk, narrow), BF),
+            pltpu.VMEM((n2, chunk, narrow), BF),
+            pltpu.VMEM((n2, chunk, narrow), BF),
+            pltpu.VMEM((chunk, narrow), BF),
+        ]
 
     packed = slots * narrow // LANES
     smem = pl.BlockSpec(memory_space=pltpu.SMEM)
@@ -476,22 +554,20 @@
             pltpu.VMEM((2, width, narrow), BF),
             pltpu.VMEM((2, width, narrow), BF),
             pltpu.VMEM((2, width, narrow), BF),
-            pltpu.VMEM((2, CHIPS_Z, chips_x, chunk, narrow), BF),
-            pltpu.VMEM((2, CHIPS_Z, chunk, narrow), BF),
-            pltpu.VMEM((2, CHIPS_Z, chunk, narrow), BF),
-            pltpu.VMEM((2, chunk, narrow), BF),
-            dma((9,)),
+            dma((7 + count,)),
             dma((6,)),
             dma((6,)),
             dma((5,)),
             dma((5,)),
-            dma((2, 6)),
-            dma((2,)),
-            dma((2, CHIPS_Z)),
-            dma((2,)),
-            dma((2, CHIPS_Z)),
-            dma((2,)),
-            dma((2,)),
+            dma((count,)),
+            dma((count, 5)),
+            dma((count,)),
+            dma((count, CHIPS_Z)),
+            dma((count,)),
+            dma((count, CHIPS_Z)),
+            dma((count,)),
+            dma((count,)),
+            *buffers,
         ],
         compiler_params=pltpu.CompilerParams(
             collective_id=0, has_side_effects=True, vmem_limit_bytes=60 * 1024 * 1024

time: 92.9 us -> 89.9 us (0.968)
  Pallas kernels: 87.1 us -> 84.2 us
    pallas_call x1, Pallas kernels: 87.1 us -> 84.2 us  [local(): pl.pallas_call(body, out_shape=(jax.ShapeDtypeStruct((masters, narrow), B...]
where the time goes in v5:
time: 89.9 us; the launch traced here: 89.8 us
  Pallas kernels  84.2 us (94%)
  other arithmetic  3.64 us (4%)
  between operations  1.3 us (1%)
    pallas_call x1, Pallas kernels, local(): pl.pallas_call(body, out_shape=(jax.ShapeDtypeStruct((masters, narrow), B...  84.2 us
    convert_element_type x1, other arithmetic, local(): return (out, *(grads[i // 2, i % 2].astype(F32) for i in range(4)))  3.64 us

profile of v5, /device:TPU:1, one launch (start us, length us, event | category | flops | bytes accessed | tf_op | source)
XLA Modules:
  0.0 89.8 jit_solution(11368655650818778833)
XLA Ops:
  1.3 84.2 %shard_map.146 = (bf16[256,256]{1,0:T(8,128)(2,1)}, bf16[2,2,1024,256]{3,2,1,0:T(8,128)(2,1)}) custom-call(s32[1,32]{1,0:T(1,128)} %refs_0_.1, s32[1]{0:T(128)S(6)} %copy.17.refs_1_, bf16[256,256]{1,0:T(8,128)(2,1)} %refs_2_.1, bf16[256,256]{1,0:T(8,128)(2,1)} %refs_3_.1, s32[1,512]{1,0:T(1,128)} %refs_4_.1, s32[1,64]{1,0:T(1,128)} %refs_5_.1, ...), custom_call_target="tpu_custom_call" | custom-call | tf_op jit(solution)/shard_map/pallas_call | solution.py:527
  85.5 0.0 copy-start
  85.5 3.6 %bitcast_convert_fusion = (f32[1024,256]{1,0:T(8,128)}, f32[1024,256]{1,0:T(8,128)}, f32[1024,256]{1,0:T(8,128)}, f32[1024,256]{1,0:T(8,128)}) fusion(bf16[2,2,1024,256]{3,2,1,0:T(8,128)(2,1)} %get-tuple-element.8), kind=kLoop, calls=%fused_computation | loop fusion | flops 1048576 | bytes 6291456 | tf_op jit(solution)/shard_map/convert_element_type | solution.py:588
  89.1 0.0 copy-done
  89.1 0.7 copy.18
Async XLA Ops:
  85.5 3.6 %copy-start = (bf16[256,256]{1,0:T(8,128)(2,1)S(1)}, bf16[256,256]{1,0:T(8,128)(2,1)}, u32[]{:S(2)}) copy-start(bf16[256,256]{1,0:T(8,128)(2,1)} %get-tuple-element.18) | copy-start | bytes 393220

commit v6 on v5

--- a/solution.py
+++ b/solution.py
@@ -122,6 +122,9 @@
             device_id_type=pl.DeviceIdType.MESH,
         )
 
+    def far_first(n):
+        return sorted(range(n), key=lambda j: -min(j, n - j))
+
     barrier = pltpu.get_barrier_semaphore()
 
     def greet(i, carry):
@@ -199,7 +202,7 @@
         return unpack(recv[n], slots)
 
     def gather_start(n, src, dst):
-        for i in range(1, hids):
+        for i in far_first(hids)[:-1]:
             remote(src, dst, ysem.at[n], yrsem.at[n], hid=lax.rem(hid + i, hids)).start()
 
     def gather_wait(n, src, dst):
@@ -259,7 +262,7 @@
     right[1] = (own_v[1] + dot(onehot_t[...], exchange_wait(3))).astype(BF)
     for h in range(hids):
         rs_send[h] = (back_f32[h] + dot_r(right[1], w_v[3, block(h)])).astype(BF)
-    for i in range(1, hids):
+    for i in far_first(hids)[:-1]:
         peer = lax.rem(hid + i, hids)
         remote(rs_send.at[peer], rs_recv.at[hid], ysem.at[2], yrsem.at[2], hid=peer).start()
 
@@ -281,9 +284,6 @@
 
     sibling = me + 1 - 2 * core
     factor = 1.0 / math.sqrt(doms * masters)
-
-    def far_first(n):
-        return sorted(range(n), key=lambda j: -min(j, n - j))
 
     class Sum:
         def __init__(self, g, m, base, rows, x_first, bufs):
@@ -434,11 +434,6 @@
     for one in early:
         one.first_start()
 
-    held = exchange_wait(4)
-    send[5] = pack(dot(adj[low, top], hid_all[hid]) + dot(adj[low, low], held), slots)
-    exchange_start(5)
-    own_v[0] = dot(adj[top, top], hid_all[hid]) + dot(adj[top, low], held)
-
     gather_wait(3, hid_all, hid_all)
     for one in late:
         for h in blocks_of(one):
@@ -446,6 +441,11 @@
         one.core_copy().start()
     for h in range(hids):
         acc[1, block(h)] = dot_t(hid_all[h], right[core])
+    held = exchange_wait(4)
+    send[5] = pack(dot(adj[low, top], hid_all[hid]) + dot(adj[low, low], held), slots)
+    exchange_start(5)
+    own_v[0] = dot(adj[top, top], hid_all[hid]) + dot(adj[top, low], held)
+
     for one in late:
         one.first_start()
     for one in early:
@@ -460,10 +460,10 @@
         one.second_start()
     for one in early:
         one.forward()
+    for one in late:
+        one.finish()
     agg_two[hid] = (own_v[0] + dot(onehot_t[...], exchange_wait(5))).astype(BF)
     gather_start(4, agg_two.at[hid], agg_two.at[hid])
-    for one in late:
-        one.finish()
     for one in late:
         one.forward()
     for one in early:

time: 89.9 us -> 92.3 us (1.027)
  Pallas kernels: 84.2 us -> 86.6 us
    pallas_call x1, Pallas kernels: 84.2 us -> 86.6 us  [local(): pl.pallas_call(body, out_shape=(jax.ShapeDtypeStruct((masters, narrow), B...]
where the time goes in v6:
time: 92.3 us; the launch traced here: 92.2 us
  Pallas kernels  86.6 us (94%)
  other arithmetic  3.64 us (4%)
  between operations  1.3 us (1%)
    pallas_call x1, Pallas kernels, local(): pl.pallas_call(body, out_shape=(jax.ShapeDtypeStruct((masters, narrow), B...  86.6 us
    convert_element_type x1, other arithmetic, local(): return (out, *(grads[i // 2, i % 2].astype(F32) for i in range(4)))  3.64 us

profile of v6, /device:TPU:1, one launch (start us, length us, event | category | flops | bytes accessed | tf_op | source)
XLA Modules:
  0.0 92.2 jit_solution(12328871229490096279)
XLA Ops:
  1.3 86.6 %shard_map.146 = (bf16[256,256]{1,0:T(8,128)(2,1)}, bf16[2,2,1024,256]{3,2,1,0:T(8,128)(2,1)}) custom-call(s32[1,32]{1,0:T(1,128)} %refs_0_.1, s32[1]{0:T(128)S(6)} %copy.17.refs_1_, bf16[256,256]{1,0:T(8,128)(2,1)} %refs_2_.1, bf16[256,256]{1,0:T(8,128)(2,1)} %refs_3_.1, s32[1,512]{1,0:T(1,128)} %refs_4_.1, s32[1,64]{1,0:T(1,128)} %refs_5_.1, ...), custom_call_target="tpu_custom_call" | custom-call | tf_op jit(solution)/shard_map/pallas_call | solution.py:527
  87.9 0.0 copy-start
  87.9 3.6 %bitcast_convert_fusion = (f32[1024,256]{1,0:T(8,128)}, f32[1024,256]{1,0:T(8,128)}, f32[1024,256]{1,0:T(8,128)}, f32[1024,256]{1,0:T(8,128)}) fusion(bf16[2,2,1024,256]{3,2,1,0:T(8,128)(2,1)} %get-tuple-element.8), kind=kLoop, calls=%fused_computation | loop fusion | flops 1048576 | bytes 6291456 | tf_op jit(solution)/shard_map/convert_element_type | solution.py:588
  91.5 0.0 copy-done
  91.5 0.7 copy.18
Async XLA Ops:
  87.9 3.6 %copy-start = (bf16[256,256]{1,0:T(8,128)(2,1)S(1)}, bf16[256,256]{1,0:T(8,128)(2,1)}, u32[]{:S(2)}) copy-start(bf16[256,256]{1,0:T(8,128)(2,1)} %get-tuple-element.18) | copy-start | bytes 393220
